TPU v7x, 32 devices: a whole 2x2x4 slice. The times are simulated.
32 devices in a mesh: band: 8 (over z, x), lev: 4 (over y, core).
Axes of the slice: x: 2, y: 2, z: 4, core: 2. Of those that a mesh axis runs over, the one named last changes fastest.
Arguments:
- spectral: bfloat16 [4, 32, 640, 640], P(None, 'lev', 'band'), may hold values from -6 to 6
- legendre_value: bfloat16 [640, 8, 640], P('band'), may hold values from -0.009765625 to 0.009765625
- legendre_slope: bfloat16 [640, 8, 640], P('band'), may hold values from -0.009765625 to 0.009765625
- wave_numbers: int32 [640], replicated, may hold values from 0 to 639, each once
- aerosol_old: bfloat16 [40, 32, 8, 2688], P(None, 'lev', 'band'), may hold values from 0 to 2
- vertical_weight: bfloat16 [3, 32, 8, 2688], P(None, 'lev', 'band'), may hold values from 0 to 0.59765625
- send_blocks: int32 [8, 5, 4], P('band'), may hold values from -1 to 20, as said below
- depart_slot: int32 [168, 4], P('band'), may hold values from 0 to 19, as said below
- depart_offset: int32 [168, 4, 128], P('band'), may hold values from 0 to 124
- depart_weight: bfloat16 [168, 4, 4, 128], P('band'), may hold values from 0 to 0.5
Outputs:
- wind_grid: bfloat16 [2, 32, 8, 2688], P(None, 'lev', 'band')
- aerosol_new: bfloat16 [40, 32, 8, 2688], P(None, 'lev', 'band')
- aerosol_flux: bfloat16 [2, 32, 8, 2688], P(None, 'lev', 'band')
Inputs may be any that keep to these rules, and one draw needn't show every extreme that they name: `send_blocks`: row b, offset o lists up to 4 of band b's own blocks (block l * 21 + c is the band's latitude l, longitudes c * 128 onward) that band b + o - 2 reads; -1 marks an empty slot; offsets toward bands that do not exist are empty; some rows are full. `depart_slot`: slot o * 4 + e of band r's pool is what band r - o + 2 lists at offset o, slot e; arrival block g belongs to band g // 21 and every slot it names is filled.
All inputs are finite; a program needn't handle non-finite values.
Results may differ from a plain program's by a relative error of at most 0.0062.
Values may be sent and summed in bfloat16 or wider, within the bound.
A program may use at most 128 MiB of HBM per device.

v0:
```python
import math

import jax
import jax.numpy as jnp
from jax import lax
from jax.sharding import PartitionSpec as P

WAVES = 640
NLON = 2688
BLK = 128


def extended(cells, sides, width):
    for axis, dim in sides:
        count = lax.axis_size(axis)
        ends = count - 1
        head = lax.slice_in_dim(cells, 0, width, axis=dim)
        tail = lax.slice_in_dim(cells, cells.shape[dim] - width, cells.shape[dim], axis=dim)
        cells = jnp.concatenate(
            [
                lax.ppermute(tail, axis, [(i, (i + 1) % count) for i in range(ends)]),
                cells,
                lax.ppermute(head, axis, [((i + 1) % count, i) for i in range(ends)]),
            ],
            axis=dim,
        )
    return cells


def shifted(value, axis, steps):
    count = lax.axis_size(axis)
    leading, last = (max(0, -steps), min(count, count - steps))
    return lax.ppermute(value, axis, [(source, source + steps) for source in range(leading, last)])


def fourier_table(wave_numbers, lon_count):
    longitudes = jnp.arange(lon_count, dtype=jnp.int32)
    phases = wave_numbers[:, None] * longitudes[None, :] % lon_count
    angles = phases.astype(jnp.float32) * (2.0 * math.pi / lon_count)
    doubled = jnp.where(wave_numbers == 0, 1.0, 2.0).astype(jnp.float32)[:, None]
    return jnp.stack([doubled * jnp.cos(angles), -doubled * jnp.sin(angles)]).astype(jnp.bfloat16)


def stencil_matrix(depart_offset, depart_weight):
    width = depart_offset.shape[-1]
    columns = jnp.arange(width, dtype=jnp.int32)
    summed = jnp.zeros(depart_offset.shape[:2] + (width, width), jnp.float32)
    for term_index in range(depart_weight.shape[2]):
        matches = columns[None, None, :, None] == depart_offset[:, :, None, :] + term_index
        summed = summed + jnp.where(
            matches, depart_weight[:, :, term_index, None, :].astype(jnp.float32), 0.0
        )
    return summed


def shards(
    spectral,
    legendre_value,
    legendre_slope,
    wave_numbers,
    aerosol_old,
    vertical_weight,
    send_blocks,
    depart_slot,
    depart_offset,
    depart_weight,
):
    band_here = lax.axis_index("band")
    wave_local = spectral.shape[2]
    own_waves = lax.dynamic_slice_in_dim(wave_numbers, band_here * wave_local, wave_local, 0)
    value_terms = jnp.einsum(
        "slj,xksj->xkls", legendre_value, spectral, preferred_element_type=jnp.float32
    )
    slope_terms = jnp.einsum(
        "slj,xksj->xkls", legendre_slope, spectral, preferred_element_type=jnp.float32
    )
    factor = own_waves.astype(jnp.float32) / WAVES
    coefficients = jnp.stack(
        [
            -slope_terms[0] - factor * value_terms[3],
            -slope_terms[1] + factor * value_terms[2],
            slope_terms[2] - factor * value_terms[1],
            slope_terms[3] + factor * value_terms[0],
        ]
    ).astype(jnp.bfloat16)
    fourier = fourier_table(wave_numbers, NLON)
    received = lax.all_to_all(coefficients, "band", split_axis=2, concat_axis=3, tiled=True)
    paired = received.reshape(2, 2, received.shape[1], received.shape[2], received.shape[3])
    wind_grid = jnp.einsum(
        "wxklm,xmi->wkli", paired, fourier, preferred_element_type=jnp.float32
    ).astype(jnp.bfloat16)
    padded = extended(aerosol_old, (("lev", 1),), 1)
    weights = vertical_weight.astype(jnp.float32)
    vertical_sum = (
        weights[0] * padded[:, :-2] + weights[1] * padded[:, 1:-1] + weights[2] * padded[:, 2:]
    )
    remapped = vertical_sum.astype(jnp.bfloat16)
    bin_count, level_count, lat_count, lon_count = remapped.shape
    block_count = lon_count // BLK
    blocks = remapped.reshape(bin_count, level_count, lat_count, block_count, BLK).transpose(
        2, 3, 0, 1, 4
    )
    blocks = blocks.reshape(lat_count * block_count, bin_count * level_count, BLK)
    listed = send_blocks[0]
    outgoing = jnp.take(blocks, jnp.clip(listed, 0, blocks.shape[0] - 1), axis=0)
    stencil = stencil_matrix(depart_offset, depart_weight).astype(jnp.bfloat16)
    offsets = listed.shape[0]
    reach_bands = offsets // 2
    pieces = []
    for offset_index in range(offsets):
        shift_by = offset_index - reach_bands
        if shift_by == 0:
            pieces.append(outgoing[offset_index])
        else:
            pieces.append(shifted(outgoing[offset_index], "band", shift_by))
    pooled = jnp.stack(pieces)
    flattened = pooled.reshape(pooled.shape[0] * pooled.shape[1], pooled.shape[2], pooled.shape[3])
    chosen = jnp.take(flattened, depart_slot, axis=0)
    block_rows = jnp.einsum("jifq,jiqp->jfp", chosen, stencil, preferred_element_type=jnp.float32)
    aerosol_new = block_rows.reshape(lat_count, block_count, bin_count, level_count, BLK).transpose(
        2, 3, 0, 1, 4
    )
    aerosol_new = aerosol_new.reshape(bin_count, level_count, lat_count, lon_count).astype(
        jnp.bfloat16
    )
    average = jnp.mean(aerosol_new.astype(jnp.float32), axis=0)
    aerosol_flux = (wind_grid.astype(jnp.float32) * average[None]).astype(jnp.bfloat16)
    return (wind_grid, aerosol_new, aerosol_flux)


def solution(mesh):
    return jax.shard_map(
        shards,
        mesh=mesh,
        in_specs=(
            P(None, "lev", "band", None),
            P("band", None, None),
            P("band", None, None),
            P(),
            P(None, "lev", "band", None),
            P(None, "lev", "band", None),
            P("band", None, None),
            P("band", None),
            P("band", None, None),
            P("band", None, None, None),
        ),
        out_specs=(
            P(None, "lev", "band", None),
            P(None, "lev", "band", None),
            P(None, "lev", "band", None),
        ),
        check_vma=False,
    )
```

profile of v0, /device:TPU:18, one launch (start us, length us, event | category | flops | bytes accessed | tf_op | source)
XLA Modules:
  0.0 116.7 jit_solution(3100503497575016621)
XLA Ops:
  0.6 0.0 copy-start
  0.6 2.7 %fusion.43 = (bf16[40,1,1,2688]{3,1,0,2:T(2,128)(2,1)S(1)}, bf16[40,1,1,2688]{3,1,0,2:T(2,128)(2,1)S(1)}) fusion(bf16[40,8,1,2688]{3,1,0,2:T(8,128)(2,1)} %bitcast.103), kind=kLoop, calls=%fused_computation.98 | loop fusion | bytes 860160 | tf_op jit(solution)/shard_map/slice | solution.py:18
  3.4 2.6 %collective-permute-start = (bf16[40,1,1,2688]{3,1,0,2:T(2,128)(2,1)S(1)}, bf16[40,1,1,2688]{3,1,0,2:T(2,128)(2,1)}, u32[]{:S(2)}, u32[]{:S(2)}) collective-permute-start(bf16[40,1,1,2688]{3,1,0,2:T(2,128)(2,1)S(1)} %get-tuple-element.18), channel_id=1, source_target_pairs={{0,1},{1,2},{2,3},{4,5},{5,6},{6,7},{8,9},{9,10},{10,11},{12,13},{... | collective-permute-start | bytes 645128 | tf_op jit(solution)/shard_map/ppermute | solution.py:21
  5.9 1.3 %collective-permute-start.1 = (bf16[40,1,1,2688]{3,1,0,2:T(2,128)(2,1)S(1)}, bf16[40,1,1,2688]{3,1,0,2:T(2,128)(2,1)}, u32[]{:S(2)}, u32[]{:S(2)}) collective-permute-start(bf16[40,1,1,2688]{3,1,0,2:T(2,128)(2,1)S(1)} %get-tuple-element.19), channel_id=1, source_target_pairs={{1,0},{2,1},{3,2},{5,4},{6,5},{7,6},{9,8},{10,9},{11,10},{13,12},{... | collective-permute-start | bytes 645128 | tf_op jit(solution)/shard_map/ppermute | solution.py:23
  7.2 0.0 copy-done
  7.2 2.9 %fusion.14 = f32[80,4,8,8]{3,2,1,0:T(8,128)S(1)} fusion(bf16[4,8,80,640]{3,2,1,0:T(8,128)(2,1)} %param.10, bf16[80,8,640]{2,1,0:T(8,128)(2,1)S(1)} %copy-done), kind=kOutput, calls=%fused_computation.29 | convolution fusion | flops 26214400 | bytes 4177920 | tf_op jit(solution)/shard_map/slj,xksj->xkls/dot_general | solution.py:74
  10.1 0.8 copy.70
  10.9 3.2 %fusion.12 = f32[80,4,8,8]{3,2,1,0:T(8,128)S(1)} fusion(bf16[4,8,80,640]{3,2,1,0:T(8,128)(2,1)} %param.10, bf16[80,8,640]{2,1,0:T(8,128)(2,1)} %param.11), kind=kOutput, calls=%fused_computation.27 | convolution fusion | flops 26214400 | bytes 4177920 | tf_op jit(solution)/shard_map/slj,xksj->xkls/dot_general | solution.py:71
  14.1 0.8 copy.72
  14.8 0.1 convert_multiply_fusion
  15.0 0.6 copy.73
  15.6 6.1 %all-to-all-start = ((bf16[4,8,8,80]{3,1,0,2:T(8,128)(2,1)}), bf16[4,8,8,80]{3,1,0,2:T(8,128)(2,1)}, u32[]{:S(2)}, u32[]{:S(2)}) async-start(bf16[4,8,8,80]{3,1,0,2:T(8,128)(2,1)} %copy.73), calls=%async_computation | async-start | bytes 131072 | tf_op jit(solution)/shard_map/all_to_all | solution.py:87
  21.9 0.1 copy.83
  22.0 0.1 reshape.248
  22.1 0.1 copy.76
  22.2 0.1 copy.84
  22.3 0.1 reshape.256
  22.4 0.1 copy.75
  22.5 32.0 %multiply_convert_fusion.1 = (bf16[1,640,2688]{2,1,0:T(8,128)(2,1)}, bf16[1,640,2688]{2,1,0:T(8,128)(2,1)}) fusion(s32[640]{0:T(1024)S(1)} %copy-done.13, f32[640]{0:T(1024)S(1)} %get-tuple-element.41, f32[640]{0:T(1024)S(1)} %get-tuple-element.42), kind=kLoop, calls=%fused_computation.9 | loop fusion | flops 22364160 | bytes 6888960 | tf_op jit(solution)/shard_map/convert.5
  54.5 0.8 slice_convert_fusion.3
  55.3 0.0 collective-permute-done
  55.3 0.0 collective-permute-done.1
  55.3 3.3 %copy_bitcast_fusion.1 = bf16[21,320,128]{2,1,0:T(8,128)(2,1)S(1)} fusion(bf16[40,8,1,2688]{3,1,0,2:T(8,128)(2,1)S(1)} %bitcast.104, bf16[40,1,1,2688]{3,1,0,2:T(2,128)(2,1)} %collective-permute-done.1, bf16[40,1,1,2688]{3,1,0,2:T(2,128)(2,1)} %collective-permute-done, f32[8,2688]{1,0:T(8,128)S(1)} %get-tuple-element.30, ...), kind=kLoop, calls=%fused_computation.44 | loop fusion | flops 12902400 | bytes 4128768 | tf_op jit(solution)/shard_map/reshape | solution.py:103
  58.6 0.0 copy-start.6
  58.6 2.0 %gather_fusion = bf16[20,320,128]{2,1,0:T(8,128)(2,1)} fusion(bf16[21,320,128]{2,1,0:T(8,128)(2,1)S(1)} %copy_bitcast_fusion.1, s32[1024]{0:T(1024)S(1)} %pad_clamp_fusion.1), kind=kCustom, calls=%fused_computation | custom fusion | bytes 3276880 | tf_op jit(solution)/shard_map/jit(_take)/gather | solution.py:105
  60.6 1.6 %broadcast_select_fusion = bf16[5,4,320,128]{3,2,1,0:T(8,128)(2,1)S(1)} fusion(bf16[5,4,320,128]{3,2,1,0:T(8,128)(2,1)} %bitcast.102, pred[5,4]{1,0:T(8,128)(4,1)S(1)} %copy.76), kind=kLoop, calls=%fused_computation.45 | loop fusion | flops 819200 | bytes 3276820 | tf_op jit(solution)/shard_map/jit(_take)/select_n | solution.py:105
  62.3 0.0 copy-start.1
  62.3 1.2 copy-done.1
  63.5 2.5 %collective-permute-start.2 = (bf16[4,320,128]{2,1,0:T(8,128)(2,1)S(1)}, bf16[4,320,128]{2,1,0:T(8,128)(2,1)S(1)}, u32[]{:S(2)}, u32[]{:S(2)}) collective-permute-start(bf16[4,320,128]{2,1,0:T(8,128)(2,1)S(1)} %get-tuple-element.24), channel_id=1, source_target_pairs={{8,0},{12,4},{16,8},{20,12},{24,16},{28,20},{9,1},{13,5},{17,9},{2... | collective-permute-start | bytes 983048 | tf_op jit(solution)/shard_map/ppermute | solution.py:33
  66.0 0.7 broadcast_add_fusion.2
  66.6 2.5 %collective-permute-start.3 = (bf16[4,320,128]{2,1,0:T(8,128)(2,1)S(1)}, bf16[4,320,128]{2,1,0:T(8,128)(2,1)S(1)}, u32[]{:S(2)}, u32[]{:S(2)}) collective-permute-start(bf16[4,320,128]{2,1,0:T(8,128)(2,1)S(1)} %get-tuple-element.23), channel_id=1, source_target_pairs={{4,0},{8,4},{12,8},{16,12},{20,16},{24,20},{28,24},{5,1},{9,5},{13... | collective-permute-start | bytes 983048 | tf_op jit(solution)/shard_map/ppermute | solution.py:33
  69.1 0.0 all-to-all-done
  69.1 0.9 copy.74
  70.0 0.7 reshape.237
  70.7 5.1 %collective-permute-done.2 = bf16[4,320,128]{2,1,0:T(8,128)(2,1)S(1)} collective-permute-done((bf16[4,320,128]{2,1,0:T(8,128)(2,1)S(1)}, bf16[4,320,128]{2,1,0:T(8,128)(2,1)S(1)}, u32[]{:S(2)}, u32[]{:S(2)}) %collective-permute-start.2) | collective-permute-done | bytes 327712 | tf_op jit(solution)/shard_map/ppermute | solution.py:33
  75.9 7.0 %collective-permute-done.3 = bf16[4,320,128]{2,1,0:T(8,128)(2,1)S(1)} collective-permute-done((bf16[4,320,128]{2,1,0:T(8,128)(2,1)S(1)}, bf16[4,320,128]{2,1,0:T(8,128)(2,1)S(1)}, u32[]{:S(2)}, u32[]{:S(2)}) %collective-permute-start.3) | collective-permute-done | bytes 327712 | tf_op jit(solution)/shard_map/ppermute | solution.py:33
  82.9 1.3 %slice_bitcast_fusion = (bf16[4,320,128]{2,1,0:T(8,128)(2,1)S(1)}, bf16[4,320,128]{2,1,0:T(8,128)(2,1)S(1)}, bf16[5,4,320,128]{3,2,1,0:T(8,128)(2,1)S(1)}) fusion(bf16[5,4,320,128]{3,2,1,0:T(8,128)(2,1)} %copy-done.1, bf16[5,4,320,128]{3,2,1,0:T(8,128)(2,1)S(1)} %bitcast_dynamic-update-slice_fusion.2), kind=kLoop, calls=%fused_computation.48 | loop fusion | bytes 1966080 | tf_op jit(solution)/shard_map/squeeze | solution.py:115
  84.2 1.9 %collective-permute-start.4 = (bf16[4,320,128]{2,1,0:T(8,128)(2,1)S(1)}, bf16[4,320,128]{2,1,0:T(8,128)(2,1)S(1)}, u32[]{:S(2)}, u32[]{:S(2)}) collective-permute-start(bf16[4,320,128]{2,1,0:T(8,128)(2,1)S(1)} %get-tuple-element.21), channel_id=1, source_target_pairs={{0,4},{4,8},{8,12},{12,16},{16,20},{20,24},{24,28},{1,5},{5,9},{9,... | collective-permute-start | bytes 983048 | tf_op jit(solution)/shard_map/ppermute | solution.py:33
  86.1 2.1 %collective-permute-start.5 = (bf16[4,320,128]{2,1,0:T(8,128)(2,1)S(1)}, bf16[4,320,128]{2,1,0:T(8,128)(2,1)S(1)}, u32[]{:S(2)}, u32[]{:S(2)}) collective-permute-start(bf16[4,320,128]{2,1,0:T(8,128)(2,1)S(1)} %get-tuple-element.20), channel_id=1, source_target_pairs={{0,8},{4,12},{8,16},{12,20},{16,24},{20,28},{1,9},{5,13},{9,17},{1... | collective-permute-start | bytes 983048 | tf_op jit(solution)/shard_map/ppermute | solution.py:33
  88.2 4.1 %fusion.11 = bf16[2,8,2688]{2,1,0:T(8,128)(2,1)S(1)} fusion(bf16[2,2,8,640]{3,2,1,0:T(8,128)(2,1)} %reshape.237, bf16[1,640,2688]{2,1,0:T(8,128)(2,1)} %get-tuple-element.40, bf16[1,640,2688]{2,1,0:T(8,128)(2,1)} %get-tuple-element.39), kind=kOutput, calls=%fused_computation.26 | convolution fusion | flops 113584128 | bytes 7008256 | tf_op jit(solution)/shard_map/wxklm,xmi->wkli/dot_general | solution.py:89
  92.4 0.0 copy-start.5
  92.4 3.4 %collective-permute-done.4 = bf16[4,320,128]{2,1,0:T(8,128)(2,1)S(1)} collective-permute-done((bf16[4,320,128]{2,1,0:T(8,128)(2,1)S(1)}, bf16[4,320,128]{2,1,0:T(8,128)(2,1)S(1)}, u32[]{:S(2)}, u32[]{:S(2)}) %collective-permute-start.4) | collective-permute-done | bytes 327712 | tf_op jit(solution)/shard_map/ppermute | solution.py:33
  95.9 5.8 %collective-permute-done.5 = bf16[4,320,128]{2,1,0:T(8,128)(2,1)S(1)} collective-permute-done((bf16[4,320,128]{2,1,0:T(8,128)(2,1)S(1)}, bf16[4,320,128]{2,1,0:T(8,128)(2,1)S(1)}, u32[]{:S(2)}, u32[]{:S(2)}) %collective-permute-start.5) | collective-permute-done | bytes 327712 | tf_op jit(solution)/shard_map/ppermute | solution.py:33
  101.8 6.5 %gather_fusion.1 = bf16[84,320,128]{2,1,0:T(8,128)(2,1)} fusion(bf16[20,320,128]{2,1,0:T(8,128)(2,1)S(1)} %bitcast.100, s32[1024]{0:T(1024)S(1)} %pad_clamp_fusion), kind=kCustom, calls=%fused_computation.1 | custom fusion | bytes 13762896 | tf_op jit(solution)/shard_map/jit(_take)/gather | solution.py:118
  108.2 0.0 copy-done.10
  108.3 6.4 %convert_reduce_fusion = (f32[21,8,128]{2,1,0:T(8,128)S(1)}, bf16[21,320,128]{2,1,0:T(8,128)(2,1)S(1)}) fusion(f32[21,4,128]{2,1,0:T(4,128)S(1)} %bitcast.110, s32[21,4,128]{2,1,0:T(4,128)S(1)} %copy-done.7, f32[21,4,128]{2,1,0:T(4,128)S(1)} %bitcast.111, s32[21,4,128]{2,1,0:T(4,128)S(1)} %copy-done.8, f32[21,4,128]{2,1,0:T(4,128)S(1)} %bitcast.109, ...), kind=kOutput, calls=%fused_computation.21 | convolution fusion | flops 903318528 | bytes 9031764 | tf_op jit(solution)/shard_map/jifq,jiqp->jfp/dot_general | solution.py:119
  114.7 1.4 %copy_bitcast_fusion = bf16[40,8,1,2688]{3,1,2,0:T(8,128)(2,1)} fusion(bf16[21,320,128]{2,1,0:T(8,128)(2,1)S(1)} %get-tuple-element.44), kind=kLoop, calls=%fused_computation.43 | loop fusion | bytes 3440640 | tf_op jit(solution)/shard_map/convert_element_type | solution.py:123
  116.1 0.7 fusion.30
  (42 shorter events, 0.4 us)
Async XLA Ops:
  0.6 6.6 %copy-start = (bf16[80,8,640]{2,1,0:T(8,128)(2,1)S(1)}, bf16[80,8,640]{2,1,0:T(8,128)(2,1)}, u32[]{:S(2)}) copy-start(bf16[80,8,640]{2,1,0:T(8,128)(2,1)} %param.12) | copy-start | bytes 2457604
  3.4 51.9 %collective-permute-start = (bf16[40,1,1,2688]{3,1,0,2:T(2,128)(2,1)S(1)}, bf16[40,1,1,2688]{3,1,0,2:T(2,128)(2,1)}, u32[]{:S(2)}, u32[]{:S(2)}) collective-permute-start(bf16[40,1,1,2688]{3,1,0,2:T(2,128)(2,1)S(1)} %get-tuple-element.18), channel_id=1, source_target_pairs={{0,1},{1,2},{2,3},{4,5},{5,6},{6,7},{8,9},{9,10},{10,11},{12,13},{... | collective-permute-start | bytes 645128 | tf_op jit(solution)/shard_map/ppermute | solution.py:21
  5.9 49.4 %collective-permute-start.1 = (bf16[40,1,1,2688]{3,1,0,2:T(2,128)(2,1)S(1)}, bf16[40,1,1,2688]{3,1,0,2:T(2,128)(2,1)}, u32[]{:S(2)}, u32[]{:S(2)}) collective-permute-start(bf16[40,1,1,2688]{3,1,0,2:T(2,128)(2,1)S(1)} %get-tuple-element.19), channel_id=1, source_target_pairs={{1,0},{2,1},{3,2},{5,4},{6,5},{7,6},{9,8},{10,9},{11,10},{13,12},{... | collective-permute-start | bytes 645128 | tf_op jit(solution)/shard_map/ppermute | solution.py:23
  10.9 3.9 %copy-start.13 = (s32[640]{0:T(1024)S(1)}, s32[640]{0:T(1024)}, u32[]{:S(2)}) copy-start(s32[640]{0:T(1024)} %param.13) | copy-start | bytes 7684
  10.9 10.8 %copy-start.14 = (s32[1,5,4]{1,2,0:T(4,128)S(1)}, s32[1,5,4]{1,2,0:T(4,128)}, u32[]{:S(2)}) copy-start(s32[1,5,4]{1,2,0:T(4,128)} %param.16) | copy-start | bytes 244
  10.9 10.9 %copy-start.15 = (s32[21,4]{0,1:T(4,128)S(1)}, s32[21,4]{0,1:T(4,128)}, u32[]{:S(2)}) copy-start(s32[21,4]{0,1:T(4,128)} %param.17) | copy-start | bytes 1012
  10.9 10.9 %copy-start.4 = (bf16[3,8,1,2688]{3,1,2,0:T(8,128)(2,1)S(1)}, bf16[3,8,1,2688]{3,1,2,0:T(8,128)(2,1)}, u32[]{:S(2)}) copy-start(bf16[3,8,1,2688]{3,1,2,0:T(8,128)(2,1)} %param.15) | copy-start | bytes 387076
  15.6 53.5 %all-to-all-start = ((bf16[4,8,8,80]{3,1,0,2:T(8,128)(2,1)}), bf16[4,8,8,80]{3,1,0,2:T(8,128)(2,1)}, u32[]{:S(2)}, u32[]{:S(2)}) async-start(bf16[4,8,8,80]{3,1,0,2:T(8,128)(2,1)} %copy.73), calls=%async_computation | async-start | bytes 131072 | tf_op jit(solution)/shard_map/all_to_all | solution.py:87
  22.5 32.0 %copy-start.3 = (bf16[21,4,4,128]{3,2,1,0:T(4,128)(2,1)S(1)}, bf16[21,4,4,128]{3,2,1,0:T(4,128)(2,1)}, u32[]{:S(2)}) copy-start(bf16[21,4,4,128]{3,2,1,0:T(4,128)(2,1)} %param.19) | copy-start | bytes 258052
  22.5 32.8 %copy-start.2 = (bf16[40,8,1,2688]{3,1,2,0:T(8,128)(2,1)S(1)}, bf16[40,8,1,2688]{3,1,2,0:T(8,128)(2,1)}, u32[]{:S(2)}) copy-start(bf16[40,8,1,2688]{3,1,2,0:T(8,128)(2,1)} %param.14) | copy-start | bytes 5160964
  58.6 7.4 %copy-start.6 = (s32[21,4,128]{2,1,0:T(4,128)S(1)}, s32[21,4,128]{2,1,0:T(4,128)}, u32[]{:S(2)}) copy-start(s32[21,4,128]{2,1,0:T(4,128)} %param.18) | copy-start | bytes 129028
  62.3 1.2 copy-start.1
  63.5 12.4 %collective-permute-start.2 = (bf16[4,320,128]{2,1,0:T(8,128)(2,1)S(1)}, bf16[4,320,128]{2,1,0:T(8,128)(2,1)S(1)}, u32[]{:S(2)}, u32[]{:S(2)}) collective-permute-start(bf16[4,320,128]{2,1,0:T(8,128)(2,1)S(1)} %get-tuple-element.24), channel_id=1, source_target_pairs={{8,0},{12,4},{16,8},{20,12},{24,16},{28,20},{9,1},{13,5},{17,9},{2... | collective-permute-start | bytes 983048 | tf_op jit(solution)/shard_map/ppermute | solution.py:33
  66.6 16.3 %collective-permute-start.3 = (bf16[4,320,128]{2,1,0:T(8,128)(2,1)S(1)}, bf16[4,320,128]{2,1,0:T(8,128)(2,1)S(1)}, u32[]{:S(2)}, u32[]{:S(2)}) collective-permute-start(bf16[4,320,128]{2,1,0:T(8,128)(2,1)S(1)} %get-tuple-element.23), channel_id=1, source_target_pairs={{4,0},{8,4},{12,8},{16,12},{20,16},{24,20},{28,24},{5,1},{9,5},{13... | collective-permute-start | bytes 983048 | tf_op jit(solution)/shard_map/ppermute | solution.py:33
  84.2 11.6 %collective-permute-start.4 = (bf16[4,320,128]{2,1,0:T(8,128)(2,1)S(1)}, bf16[4,320,128]{2,1,0:T(8,128)(2,1)S(1)}, u32[]{:S(2)}, u32[]{:S(2)}) collective-permute-start(bf16[4,320,128]{2,1,0:T(8,128)(2,1)S(1)} %get-tuple-element.21), channel_id=1, source_target_pairs={{0,4},{4,8},{8,12},{12,16},{16,20},{20,24},{24,28},{1,5},{5,9},{9,... | collective-permute-start | bytes 983048 | tf_op jit(solution)/shard_map/ppermute | solution.py:33
  86.1 15.5 %collective-permute-start.5 = (bf16[4,320,128]{2,1,0:T(8,128)(2,1)S(1)}, bf16[4,320,128]{2,1,0:T(8,128)(2,1)S(1)}, u32[]{:S(2)}, u32[]{:S(2)}) collective-permute-start(bf16[4,320,128]{2,1,0:T(8,128)(2,1)S(1)} %get-tuple-element.20), channel_id=1, source_target_pairs={{0,8},{4,12},{8,16},{12,20},{16,24},{20,28},{1,9},{5,13},{9,17},{1... | collective-permute-start | bytes 983048 | tf_op jit(solution)/shard_map/ppermute | solution.py:33
  92.4 23.7 %copy-start.5 = (bf16[2,8,2688]{2,1,0:T(8,128)(2,1)}, bf16[2,8,2688]{2,1,0:T(8,128)(2,1)S(1)}, u32[]{:S(2)}) copy-start(bf16[2,8,2688]{2,1,0:T(8,128)(2,1)S(1)} %fusion.11) | copy-start | bytes 258052
  101.7 6.5 %copy-start.7 = (s32[21,4,128]{2,1,0:T(4,128)S(1)}, s32[21,4,128]{2,1,0:T(4,128)}, u32[]{:S(2)}) copy-start(s32[21,4,128]{2,1,0:T(4,128)} %get-tuple-element.37) | copy-start | bytes 129028
  101.7 6.5 %copy-start.8 = (s32[21,4,128]{2,1,0:T(4,128)S(1)}, s32[21,4,128]{2,1,0:T(4,128)}, u32[]{:S(2)}) copy-start(s32[21,4,128]{2,1,0:T(4,128)} %get-tuple-element.38) | copy-start | bytes 129028
  101.7 6.5 %copy-start.9 = (f32[21,4,1,128]{3,2,1,0:T(1,128)S(1)}, f32[21,4,1,128]{3,2,1,0:T(1,128)}, u32[]{:S(2)}) copy-start(f32[21,4,1,128]{3,2,1,0:T(1,128)} %get-tuple-element.32) | copy-start | bytes 129028
  101.7 6.5 %copy-start.10 = (f32[21,4,1,128]{3,2,1,0:T(1,128)S(1)}, f32[21,4,1,128]{3,2,1,0:T(1,128)}, u32[]{:S(2)}) copy-start(f32[21,4,1,128]{3,2,1,0:T(1,128)} %get-tuple-element.33) | copy-start | bytes 129028
  101.8 6.5 %copy-start.11 = (f32[21,4,1,128]{3,2,1,0:T(1,128)S(1)}, f32[21,4,1,128]{3,2,1,0:T(1,128)}, u32[]{:S(2)}) copy-start(f32[21,4,1,128]{3,2,1,0:T(1,128)} %get-tuple-element.34) | copy-start | bytes 129028
  101.8 6.5 %copy-start.12 = (f32[21,4,1,128]{3,2,1,0:T(1,128)S(1)}, f32[21,4,1,128]{3,2,1,0:T(1,128)}, u32[]{:S(2)}) copy-start(f32[21,4,1,128]{3,2,1,0:T(1,128)} %get-tuple-element.35) | copy-start | bytes 129028
where the time goes:
time: 117 us
  other arithmetic  39.2 us (34%)
  waiting for transfers between devices  21.4 us (18%)
  local copies, waits for them, and re-layouts  19.6 us (17%)
  starting transfers between devices  18.9 us (16%)
  matrix products  16.6 us (14%)
    another operation x2, other arithmetic  32 us
    ppermute x4, waiting for transfers between devices, shifted(): lax.ppermute(value, axis, [(source, source + steps) for source in range(l...  21.4 us
    ppermute x4, starting transfers between devices, shifted(): lax.ppermute(value, axis, [(source, source + steps) for source in range(l...  8.95 us
    gather x1, local copies, waits for them, and re-layouts, shards(): chosen = jnp.take(flattened, depart_slot, axis=0)  6.45 us
    dot_general x1, matrix products, shards(): jnp.einsum('jifq,jiqp->jfp', chosen, stencil, preferred_element_type=jnp....  6.41 us
    all_to_all x1, starting transfers between devices, shards(): lax.all_to_all(coefficients, 'band', split_axis=2, concat_axis=3, tiled=T...  6.11 us
    dot_general x1, matrix products, shards(): jnp.einsum('wxklm,xmi->wkli', paired, fourier, preferred_element_type=jnp...  4.14 us
    reshape x1, other arithmetic, shards(): blocks.reshape(lat_count * block_count, bin_count * level_count, BLK)  3.29 us
  transfers between devices with their start and end apart: 7, of which 4 were waited for; matrix products, arithmetic and copies ran while one was open for 47% of the time, Pallas kernels for 0%

commit v1 on v0

v1 whole, which is shorter than its diff:
```python
import functools
import math

import jax
import jax.numpy as jnp
from jax import lax
from jax.experimental import pallas as pl
from jax.experimental.pallas import tpu as pltpu
from jax.sharding import PartitionSpec as P

WAVES = 640
NLON = 2688
BLK = 128
GROUP = 16
LANES = 128
LIMIT = 48 * 2**20
VMEM = pl.BlockSpec(memory_space=pltpu.VMEM)
SMEM = pl.BlockSpec(memory_space=pltpu.SMEM)


def shifted(value, axis, steps):
    count = lax.axis_size(axis)
    leading, last = (max(0, -steps), min(count, count - steps))
    return lax.ppermute(value, axis, [(source, source + steps) for source in range(leading, last)])


def padded_to(value, axis, multiple):
    extra = -value.shape[axis] % multiple
    if extra == 0:
        return value
    widths = [(0, 0)] * value.ndim
    widths[axis] = (0, extra)
    return jnp.pad(value, widths)


def legendre_kernel(lat_count, level_count, spec_ref, val_ref, slope_ref, factor_ref, out_ref, acc):
    step = pl.program_id(0)
    rows = spec_ref.shape[0]
    cols = GROUP * lat_count
    spec = spec_ref[...].reshape(rows * GROUP, spec_ref.shape[2])
    own = lax.broadcasted_iota(jnp.int32, (GROUP, cols), 0)
    col = lax.broadcasted_iota(jnp.int32, (GROUP, cols), 1)
    keep = (col // lat_count == own)[None]

    def terms(table_ref):
        table = table_ref[...].reshape(cols, table_ref.shape[2])
        product = lax.dot_general(
            spec, table, (((1,), (1,)), ((), ())), preferred_element_type=jnp.float32
        )
        product = product.reshape(rows, GROUP, cols)
        return jnp.sum(jnp.where(keep, product, 0.0), axis=1)

    value = terms(val_ref)
    slope = terms(slope_ref)
    factor = factor_ref[0]
    k = level_count
    v = [value[x * k : (x + 1) * k] for x in range(4)]
    d = [slope[x * k : (x + 1) * k] for x in range(4)]
    coefficients = jnp.concatenate(
        [
            -d[0] - factor * v[3],
            -d[1] + factor * v[2],
            d[2] - factor * v[1],
            d[3] + factor * v[0],
        ],
        axis=0,
    ).astype(jnp.bfloat16)
    width = acc.shape[1]
    lanes = width // lat_count
    row = lax.broadcasted_iota(jnp.int32, (cols, width), 0)
    lane = lax.broadcasted_iota(jnp.int32, (cols, width), 1)
    slot = lane % lanes - step * GROUP
    hot = ((slot * lat_count + lane // lanes == row) & (slot >= 0) & (slot < GROUP)).astype(
        jnp.float32
    ).astype(jnp.bfloat16)
    part = jnp.dot(coefficients, hot, preferred_element_type=jnp.float32)

    @pl.when(step == 0)
    def _():
        acc[...] = part

    @pl.when(step > 0)
    def _():
        acc[...] += part

    @pl.when(step == pl.num_programs(0) - 1)
    def _():
        for lat in range(lat_count):
            out_ref[lat] = acc[:, lat * lanes : (lat + 1) * lanes].astype(jnp.bfloat16)


def wind_coefficients(spectral, legendre_value, legendre_slope, own_waves):
    fields, level_count, wave_local, trunc = spectral.shape
    lat_count = legendre_value.shape[1]
    rows = fields * level_count
    spec = padded_to(spectral.reshape(rows, wave_local, trunc), 1, GROUP)
    value = padded_to(legendre_value, 0, GROUP)
    slope = padded_to(legendre_slope, 0, GROUP)
    steps = spec.shape[1] // GROUP
    lanes = -(-spec.shape[1] // LANES) * LANES
    factor = padded_to(own_waves.astype(jnp.float32) / WAVES, 0, GROUP)
    factor = jnp.broadcast_to(factor[:, None], (factor.shape[0], lat_count))
    factor = factor.reshape(steps, 1, GROUP * lat_count)
    table = pl.BlockSpec((GROUP, lat_count, trunc), lambda g: (g, 0, 0))
    return pl.pallas_call(
        functools.partial(legendre_kernel, lat_count, level_count),
        out_shape=jax.ShapeDtypeStruct((lat_count, rows, lanes), jnp.bfloat16),
        grid=(steps,),
        in_specs=[
            pl.BlockSpec((rows, GROUP, trunc), lambda g: (0, g, 0)),
            table,
            table,
            pl.BlockSpec((1, 1, GROUP * lat_count), lambda g: (g, 0, 0)),
        ],
        out_specs=pl.BlockSpec((lat_count, rows, lanes), lambda g: (0, 0, 0)),
        scratch_shapes=[pltpu.VMEM((rows, lat_count * lanes), jnp.float32)],
        compiler_params=pltpu.CompilerParams(vmem_limit_bytes=LIMIT),
        cost_estimate=pl.CostEstimate(
            flops=2 * rows * GROUP * 2 * GROUP * lat_count * trunc * steps,
            bytes_accessed=5_000_000,
            transcendentals=0,
        ),
    )(spec, value, slope, factor)


def wind_kernel(received_ref, cos_block_ref, sin_block_ref, table_ref, wind_ref, lhs):
    shard_count = received_ref.shape[0]
    level_count = wind_ref.shape[1]
    k = level_count
    whole = jnp.concatenate([received_ref[b] for b in range(shard_count)], axis=1)
    whole = whole.astype(jnp.float32)
    real = jnp.concatenate([whole[0:k], whole[2 * k : 3 * k]], axis=0)
    imag = jnp.concatenate([whole[k : 2 * k], whole[3 * k : 4 * k]], axis=0)
    width = whole.shape[1]
    block_count = cos_block_ref.shape[0]
    for c in range(block_count):
        cos_c = cos_block_ref[c : c + 1, :]
        sin_c = sin_block_ref[c : c + 1, :]
        at = slice(c * 2 * k, (c + 1) * 2 * k)
        lhs[at, 0:width] = (real * cos_c - imag * sin_c).astype(jnp.bfloat16)
        lhs[at, width : 2 * width] = (-real * sin_c - imag * cos_c).astype(jnp.bfloat16)
    grid = jnp.dot(lhs[...], table_ref[...], preferred_element_type=jnp.float32)
    grid = grid.astype(jnp.bfloat16)
    for c in range(block_count):
        for w in range(2):
            start = (2 * c + w) * k
            wind_ref[w, :, c * BLK : (c + 1) * BLK] = grid[start : start + k]


def angle_tables(wave_numbers, shard_count, lanes, block_count):
    waves = padded_to(wave_numbers.reshape(shard_count, -1), 1, lanes).reshape(-1)
    scale = 2.0 * math.pi / NLON
    doubled = jnp.where(waves == 0, 1.0, 2.0).astype(jnp.float32)
    starts = jnp.arange(block_count, dtype=jnp.int32) * BLK
    coarse = (starts[:, None] * waves[None, :] % NLON).astype(jnp.float32) * scale
    fine = jnp.arange(BLK, dtype=jnp.int32)
    fine = (waves[:, None] * fine[None, :] % NLON).astype(jnp.float32) * scale
    table = jnp.concatenate([jnp.cos(fine), jnp.sin(fine)], axis=0).astype(jnp.bfloat16)
    return doubled * jnp.cos(coarse), doubled * jnp.sin(coarse), table


def winds(received, cos_block, sin_block, table, level_count, lon_count):
    block_count = lon_count // BLK
    width = table.shape[0]
    return pl.pallas_call(
        wind_kernel,
        out_shape=jax.ShapeDtypeStruct((2, level_count, lon_count), jnp.bfloat16),
        in_specs=[VMEM] * 4,
        out_specs=VMEM,
        scratch_shapes=[pltpu.VMEM((block_count * 2 * level_count, width), jnp.bfloat16)],
        compiler_params=pltpu.CompilerParams(vmem_limit_bytes=LIMIT),
        cost_estimate=pl.CostEstimate(
            flops=2 * block_count * 2 * level_count * width * BLK,
            bytes_accessed=2_000_000,
            transcendentals=0,
        ),
    )(received, cos_block, sin_block, table)


def remap_kernel(offsets, slots, listed_ref, old_ref, below_ref, above_ref, weight_ref, *out_refs):
    level_count = old_ref.shape[1]
    block_count = old_ref.shape[2] // BLK
    level = lax.broadcasted_iota(jnp.int32, (1, level_count, BLK), 1)
    for o in range(offsets):
        for e in range(slots):
            block = jnp.clip(listed_ref[o * slots + e], 0, block_count - 1)
            lons = pl.ds(pl.multiple_of(block * BLK, BLK), BLK)
            weights = weight_ref[:, :, lons].astype(jnp.float32)
            old = old_ref[:, :, lons].astype(jnp.float32)
            below = below_ref[:, :, lons].astype(jnp.float32)
            above = above_ref[:, :, lons].astype(jnp.float32)
            lower = jnp.where(level == 0, below, pltpu.roll(old, 1, 1))
            upper = jnp.where(
                level == level_count - 1, above, pltpu.roll(old, level_count - 1, 1)
            )
            summed = weights[0:1] * lower + weights[1:2] * old + weights[2:3] * upper
            out_refs[o][e] = summed.astype(jnp.bfloat16)


def remapped_blocks(listed, old, below, above, weight):
    offsets, slots = listed.shape
    bin_count, level_count, _ = old.shape
    piece = jax.ShapeDtypeStruct((slots, bin_count, level_count, BLK), jnp.bfloat16)
    return pl.pallas_call(
        functools.partial(remap_kernel, offsets, slots),
        out_shape=[piece] * offsets,
        in_specs=[SMEM] + [VMEM] * 4,
        out_specs=[VMEM] * offsets,
        compiler_params=pltpu.CompilerParams(vmem_limit_bytes=LIMIT),
        cost_estimate=pl.CostEstimate(
            flops=10 * old.size, bytes_accessed=4_000_000, transcendentals=0
        ),
    )(listed.reshape(-1), old, below, above, weight)


def arrive_kernel(offsets, slots, depart_ref, start_ref, weight_ref, wind_ref, *refs):
    pool_refs = refs[:offsets]
    new_ref, flux_ref, pool = refs[offsets:]
    block = pl.program_id(0)
    bin_count, level_count, width = new_ref.shape
    rows = bin_count * level_count

    @pl.when(block == 0)
    def _():
        for o in range(offsets):
            for e in range(slots):
                pool[o * slots + e] = pool_refs[o][e].reshape(rows, width)

    stencil_rows = start_ref.shape[1]
    points = weight_ref.shape[2]
    q = lax.broadcasted_iota(jnp.int32, (width, width), 0)
    taken, matrices = [], []
    for t in range(stencil_rows):
        away = q - start_ref[0, t : t + 1, :]
        weights = weight_ref[0, t].astype(jnp.float32)
        matrix = jnp.zeros((width, width), jnp.float32)
        for u in range(points):
            matrix = jnp.where(away == u, weights[u : u + 1, :], matrix)
        matrices.append(matrix.astype(jnp.bfloat16))
        taken.append(pool[depart_ref[block * stencil_rows + t]])
    lhs = jnp.concatenate(taken, axis=1)
    rhs = jnp.concatenate(matrices, axis=0)
    new = jnp.dot(lhs, rhs, preferred_element_type=jnp.float32).astype(jnp.bfloat16)
    new = new.reshape(bin_count, level_count, width)
    new_ref[...] = new
    average = jnp.sum(new.astype(jnp.float32), axis=0) / bin_count
    flux_ref[...] = (wind_ref[...].astype(jnp.float32) * average[None]).astype(jnp.bfloat16)


def arrivals(depart_slot, depart_offset, depart_weight, wind, pieces):
    offsets = len(pieces)
    slots, bin_count, level_count, _ = pieces[0].shape
    block_count, stencil_rows = depart_slot.shape
    lon_count = wind.shape[2]
    rows = bin_count * level_count
    points = depart_weight.shape[2]
    two = pl.BlockSpec((2, level_count, BLK), lambda c: (0, 0, c))
    return pl.pallas_call(
        functools.partial(arrive_kernel, offsets, slots),
        out_shape=[
            jax.ShapeDtypeStruct((bin_count, level_count, lon_count), jnp.bfloat16),
            jax.ShapeDtypeStruct((2, level_count, lon_count), jnp.bfloat16),
        ],
        grid=(block_count,),
        in_specs=[
            SMEM,
            pl.BlockSpec((1, stencil_rows, BLK), lambda c: (c, 0, 0)),
            pl.BlockSpec((1, stencil_rows, points, BLK), lambda c: (c, 0, 0, 0)),
            two,
        ]
        + [VMEM] * offsets,
        out_specs=[pl.BlockSpec((bin_count, level_count, BLK), lambda c: (0, 0, c)), two],
        scratch_shapes=[pltpu.VMEM((offsets * slots, rows, BLK), jnp.bfloat16)],
        compiler_params=pltpu.CompilerParams(vmem_limit_bytes=LIMIT),
        cost_estimate=pl.CostEstimate(
            flops=2 * block_count * stencil_rows * rows * BLK * BLK,
            bytes_accessed=4_000_000,
            transcendentals=0,
        ),
    )(depart_slot.reshape(-1), depart_offset, depart_weight, wind, *pieces)


def shards(
    spectral,
    legendre_value,
    legendre_slope,
    wave_numbers,
    aerosol_old,
    vertical_weight,
    send_blocks,
    depart_slot,
    depart_offset,
    depart_weight,
):
    band_here = lax.axis_index("band")
    band_count = lax.axis_size("band")
    wave_local = spectral.shape[2]
    bin_count, level_count, lat_count, lon_count = aerosol_old.shape
    old = aerosol_old.reshape(bin_count, level_count, lon_count)
    weight = vertical_weight.reshape(3, level_count, lon_count)
    below = shifted(old[:, level_count - 1 :], "lev", 1)
    above = shifted(old[:, :1], "lev", -1)

    own_waves = lax.dynamic_slice_in_dim(wave_numbers, band_here * wave_local, wave_local, 0)
    coefficients = wind_coefficients(spectral, legendre_value, legendre_slope, own_waves)
    received = lax.all_to_all(coefficients, "band", split_axis=0, concat_axis=0, tiled=True)
    cos_block, sin_block, table = angle_tables(
        wave_numbers, band_count, coefficients.shape[2], lon_count // BLK
    )

    outgoing = remapped_blocks(send_blocks[0], old, below, above, weight)
    reach_bands = len(outgoing) // 2
    pieces = [
        piece if index == reach_bands else shifted(piece, "band", index - reach_bands)
        for index, piece in enumerate(outgoing)
    ]
    wind = winds(received, cos_block, sin_block, table, level_count, lon_count)
    new, flux = arrivals(depart_slot, depart_offset, depart_weight, wind, pieces)
    lat_shape = (level_count, lat_count, lon_count)
    return (
        wind.reshape((2, *lat_shape)),
        new.reshape((bin_count, *lat_shape)),
        flux.reshape((2, *lat_shape)),
    )


def solution(mesh):
    return jax.shard_map(
        shards,
        mesh=mesh,
        in_specs=(
            P(None, "lev", "band", None),
            P("band", None, None),
            P("band", None, None),
            P(),
            P(None, "lev", "band", None),
            P(None, "lev", "band", None),
            P("band", None, None),
            P("band", None),
            P("band", None, None),
            P("band", None, None, None),
        ),
        out_specs=(
            P(None, "lev", "band", None),
            P(None, "lev", "band", None),
            P(None, "lev", "band", None),
        ),
        check_vma=False,
    )
```

time: 117 us -> 68 us (0.58)
  the two profiles are of different devices: /device:TPU:18 before, /device:TPU:19 now
where the time goes in v1:
time: 68 us; the launch traced here: 67.4 us
  starting transfers between devices  22.1 us (32%)
  Pallas kernels  19.5 us (29%)
  waiting for transfers between devices  12.2 us (18%)
  local copies, waits for them, and re-layouts  8.98 us (13%)
  other arithmetic  3.89 us (6%)
  between operations  0.79 us (1%)
    ppermute x6, starting transfers between devices, shifted(): lax.ppermute(value, axis, [(source, source + steps) for source in range(l...  16.5 us
    ppermute x6, waiting for transfers between devices, shifted(): lax.ppermute(value, axis, [(source, source + steps) for source in range(l...  12.1 us
    pallas_call x1, Pallas kernels, arrivals(): pl.pallas_call(functools.partial(arrive_kernel, offsets, slots), out_shap...  11.1 us
    unnamed x28, local copies, waits for them, and re-layouts  7.02 us
    all_to_all x1, starting transfers between devices, shards(): lax.all_to_all(coefficients, 'band', split_axis=0, concat_axis=0, tiled=T...  5.68 us
    pallas_call x1, Pallas kernels, wind_coefficients(): pl.pallas_call(functools.partial(legendre_kernel, lat_count, level_count)...  4.27 us
    pallas_call x1, Pallas kernels, remapped_blocks(): pl.pallas_call(functools.partial(remap_kernel, offsets, slots), out_shape...  2.94 us
    another operation x1, other arithmetic  2.58 us
  transfers between devices with their start and end apart: 7, of which 5 were waited for; matrix products, arithmetic and copies ran while one was open for 7% of the time, Pallas kernels for 6%

profile of v1, /device:TPU:19, one launch (start us, length us, event | category | flops | bytes accessed | tf_op | source)
XLA Modules:
  0.0 67.4 jit_solution(14648773378482339299)
XLA Ops:
  0.6 0.8 %convert_multiply_fusion = f32[80]{0:T(128)S(1)} fusion(s32[640]{0:T(1024)} %param.13, s32[]{:T(128)S(6)} %select_n.24), kind=kLoop, calls=%fused_computation.22 | loop fusion | flops 160 | bytes 644 | tf_op jit(solution)/shard_map/div | solution.py:101
  1.4 0.1 broadcast_in_dim.22
  1.5 0.1 broadcast_in_dim.23
  1.6 0.1 broadcast_in_dim.27.factor_ref
  1.7 0.0 copy-start.1
  1.7 1.9 %copy-done.1 = bf16[4,8,80,640]{3,2,1,0:T(8,128)(2,1)S(1)} copy-done((bf16[4,8,80,640]{3,2,1,0:T(8,128)(2,1)S(1)}, bf16[4,8,80,640]{3,2,1,0:T(8,128)(2,1)}, u32[]{:S(2)}) %copy-start.1) | copy-done | bytes 3276824
  3.6 0.0 copy-start.2
  3.6 1.1 %copy-done.2 = bf16[80,8,640]{2,1,0:T(8,128)(2,1)S(1)} copy-done((bf16[80,8,640]{2,1,0:T(8,128)(2,1)S(1)}, bf16[80,8,640]{2,1,0:T(8,128)(2,1)}, u32[]{:S(2)}) %copy-start.2) | copy-done | bytes 819224
  4.7 0.0 copy-start.3
  4.7 1.1 %copy-done.3 = bf16[80,8,640]{2,1,0:T(8,128)(2,1)S(1)} copy-done((bf16[80,8,640]{2,1,0:T(8,128)(2,1)S(1)}, bf16[80,8,640]{2,1,0:T(8,128)(2,1)}, u32[]{:S(2)}) %copy-start.3) | copy-done | bytes 819224
  5.9 4.3 %shard_map.121 = bf16[8,32,128]{2,1,0:T(8,128)(2,1)} custom-call(bf16[32,80,640]{2,1,0:T(8,128)(2,1)S(1)} %bitcast.18, bf16[80,8,640]{2,1,0:T(8,128)(2,1)S(1)} %copy-done.2, bf16[80,8,640]{2,1,0:T(8,128)(2,1)S(1)} %copy-done.3, f32[5,1,128]{2,1,0:T(1,128)S(1)} %broadcast_in_dim.27.factor_ref), custom_call_target="tpu_custom_call" | custom-call | flops 838860800 | bytes 5000000 | tf_op jit(solution)/shard_map/pallas_call | solution.py:105
  10.2 0.0 copy-start.10
  10.2 5.7 %all-to-all-start = ((bf16[8,32,128]{2,1,0:T(8,128)(2,1)}), bf16[8,32,128]{2,1,0:T(8,128)(2,1)S(1)}, u32[]{:S(2)}, u32[]{:S(2)}) async-start(bf16[8,32,128]{2,1,0:T(8,128)(2,1)} %shard_map.121), calls=%async_computation | async-start | bytes 131072 | tf_op jit(solution)/shard_map/all_to_all | solution.py:306
  15.8 0.0 copy-done
  15.8 1.5 %fusion.10 = (bf16[40,1,2688]{2,1,0:T(2,128)(2,1)}, bf16[40,1,2688]{2,1,0:T(2,128)(2,1)}) fusion(bf16[40,8,2688]{2,1,0:T(8,128)(2,1)S(1)} %bitcast.16), kind=kLoop, calls=%fused_computation.23 | loop fusion | bytes 860160 | tf_op jit(solution)/shard_map/slice | solution.py:302
  17.3 3.1 %collective-permute-start.1 = (bf16[40,1,2688]{2,1,0:T(2,128)(2,1)}, bf16[40,1,2688]{2,1,0:T(2,128)(2,1)S(1)}, u32[]{:S(2)}, u32[]{:S(2)}) collective-permute-start(bf16[40,1,2688]{2,1,0:T(2,128)(2,1)} %get-tuple-element.23), channel_id=1, source_target_pairs={{1,0},{2,1},{3,2},{5,4},{6,5},{7,6},{9,8},{10,9},{11,10},{13,12},{... | collective-permute-start | bytes 645128 | tf_op jit(solution)/shard_map/ppermute | solution.py:24
  20.4 3.0 %collective-permute-start = (bf16[40,1,2688]{2,1,0:T(2,128)(2,1)}, bf16[40,1,2688]{2,1,0:T(2,128)(2,1)S(1)}, u32[]{:S(2)}, u32[]{:S(2)}) collective-permute-start(bf16[40,1,2688]{2,1,0:T(2,128)(2,1)} %get-tuple-element.24), channel_id=1, source_target_pairs={{0,1},{1,2},{2,3},{4,5},{5,6},{6,7},{8,9},{9,10},{10,11},{12,13},{... | collective-permute-start | bytes 645128 | tf_op jit(solution)/shard_map/ppermute | solution.py:24
  23.5 0.0 copy-done.10
  23.5 0.1 reshape.56
  23.6 0.0 copy-done.11
  23.6 0.1 copy.20
  23.7 0.1 reshape_squeeze.3.listed_ref
  23.8 2.6 %cosine_convert_fusion = (bf16[1024,128]{1,0:T(8,128)(2,1)S(1)}, bf16[1024,128]{1,0:T(8,128)(2,1)S(1)}) fusion(s32[1024]{0:T(1024)S(1)} %pad_bitcast_fusion), kind=kLoop, calls=%fused_computation.5 | loop fusion | flops 1441792 | bytes 528384 | tf_op jit(solution)/shard_map/convert
  26.4 0.0 copy-start.12
  26.4 1.2 %collective-permute-done.1.above_ref = bf16[40,1,2688]{2,1,0:T(2,128)(2,1)S(1)} collective-permute-done((bf16[40,1,2688]{2,1,0:T(2,128)(2,1)}, bf16[40,1,2688]{2,1,0:T(2,128)(2,1)S(1)}, u32[]{:S(2)}, u32[]{:S(2)}) %collective-permute-start.1) | collective-permute-done | bytes 215072 | tf_op jit(solution)/shard_map/ppermute | solution.py:24
  27.6 1.3 %collective-permute-done.below_ref = bf16[40,1,2688]{2,1,0:T(2,128)(2,1)S(1)} collective-permute-done((bf16[40,1,2688]{2,1,0:T(2,128)(2,1)}, bf16[40,1,2688]{2,1,0:T(2,128)(2,1)S(1)}, u32[]{:S(2)}, u32[]{:S(2)}) %collective-permute-start) | collective-permute-done | bytes 215072 | tf_op jit(solution)/shard_map/ppermute | solution.py:24
  28.9 0.0 copy-done.4
  28.9 2.9 %shard_map.123 = (bf16[4,40,8,128]{3,2,1,0:T(8,128)(2,1)}, bf16[4,40,8,128]{3,2,1,0:T(8,128)(2,1)}, bf16[4,40,8,128]{3,2,1,0:T(8,128)(2,1)S(1)}, bf16[4,40,8,128]{3,2,1,0:T(8,128)(2,1)}, bf16[4,40,8,128]{3,2,1,0:T(8,128)(2,1)}) custom-call(s32[20]{0:T(128)S(1)} %reshape_squeeze.3.listed_ref, bf16[40,8,2688]{2,1,0:T(8,128)(2,1)S(1)} %bitcast.17, ...), custom_call_target="tpu_custom_call" | custom-call | flops 8601600 | bytes 4000000 | tf_op jit(solution)/shard_map/pallas_call | solution.py:204
  31.9 0.7 %copy-done.6 = bf16[4,40,8,128]{3,2,1,0:T(8,128)(2,1)} copy-done((bf16[4,40,8,128]{3,2,1,0:T(8,128)(2,1)}, bf16[4,40,8,128]{3,2,1,0:T(8,128)(2,1)S(1)}, u32[]{:S(2)}) %copy-start.6) | copy-done | bytes 327704
  32.6 2.2 %collective-permute-start.2 = (bf16[4,40,8,128]{3,2,1,0:T(8,128)(2,1)}, bf16[4,40,8,128]{3,2,1,0:T(8,128)(2,1)S(1)}, u32[]{:S(2)}, u32[]{:S(2)}) collective-permute-start(bf16[4,40,8,128]{3,2,1,0:T(8,128)(2,1)} %get-tuple-element.10), channel_id=1, source_target_pairs={{8,0},{12,4},{16,8},{20,12},{24,16},{28,20},{9,1},{13,5},{17,9},{2... | collective-permute-start | bytes 983048 | tf_op jit(solution)/shard_map/ppermute | solution.py:24
  34.8 2.2 %collective-permute-start.3 = (bf16[4,40,8,128]{3,2,1,0:T(8,128)(2,1)}, bf16[4,40,8,128]{3,2,1,0:T(8,128)(2,1)S(1)}, u32[]{:S(2)}, u32[]{:S(2)}) collective-permute-start(bf16[4,40,8,128]{3,2,1,0:T(8,128)(2,1)} %get-tuple-element.11), channel_id=1, source_target_pairs={{4,0},{8,4},{12,8},{16,12},{20,16},{24,20},{28,24},{5,1},{9,5},{13... | collective-permute-start | bytes 983048 | tf_op jit(solution)/shard_map/ppermute | solution.py:24
  37.0 4.0 %collective-permute-start.4 = (bf16[4,40,8,128]{3,2,1,0:T(8,128)(2,1)}, bf16[4,40,8,128]{3,2,1,0:T(8,128)(2,1)S(1)}, u32[]{:S(2)}, u32[]{:S(2)}) collective-permute-start(bf16[4,40,8,128]{3,2,1,0:T(8,128)(2,1)} %get-tuple-element.13), channel_id=1, source_target_pairs={{0,4},{4,8},{8,12},{12,16},{16,20},{20,24},{24,28},{1,5},{5,9},{9,... | collective-permute-start | bytes 983048 | tf_op jit(solution)/shard_map/ppermute | solution.py:24
  41.0 1.9 %collective-permute-start.5 = (bf16[4,40,8,128]{3,2,1,0:T(8,128)(2,1)}, bf16[4,40,8,128]{3,2,1,0:T(8,128)(2,1)S(1)}, u32[]{:S(2)}, u32[]{:S(2)}) collective-permute-start(bf16[4,40,8,128]{3,2,1,0:T(8,128)(2,1)} %get-tuple-element.14), channel_id=1, source_target_pairs={{0,8},{4,12},{8,16},{12,20},{16,24},{20,28},{1,9},{5,13},{9,17},{1... | collective-permute-start | bytes 983048 | tf_op jit(solution)/shard_map/ppermute | solution.py:24
  42.9 0.5 sine_multiply_fusion
  43.4 0.0 copy-done.12
  43.4 0.1 copy.19
  43.5 0.1 reshape.59.depart_ref
  43.6 0.0 all-to-all-done.received_ref
  43.6 1.2 %shard_map.122.wind_ref = bf16[2,8,2688]{2,1,0:T(8,128)(2,1)} custom-call(bf16[8,32,128]{2,1,0:T(8,128)(2,1)S(1)} %all-to-all-done.received_ref, f32[21,1024]{1,0:T(8,128)S(1)} %get-tuple-element.26.cos_block_ref, f32[21,1024]{1,0:T(8,128)S(1)} %get-tuple-element.25.sin_block_ref, bf16[2048,128]{1,0:T(8,128)(2,1)S(1)} %pad_maximum_fusion.table_ref), custom_call_target="tpu_custom_call" | custom-call | flops 176160768 | bytes 2000000 | tf_op jit(solution)/shard_map/pallas_call | solution.py:165
  44.8 0.0 collective-permute-done.2.refs_0_
  44.8 4.7 %collective-permute-done.3.refs_1_ = bf16[4,40,8,128]{3,2,1,0:T(8,128)(2,1)S(1)} collective-permute-done((bf16[4,40,8,128]{3,2,1,0:T(8,128)(2,1)}, bf16[4,40,8,128]{3,2,1,0:T(8,128)(2,1)S(1)}, u32[]{:S(2)}, u32[]{:S(2)}) %collective-permute-start.3) | collective-permute-done | bytes 327712 | tf_op jit(solution)/shard_map/ppermute | solution.py:24
  49.5 3.7 %collective-permute-done.4.refs_3_ = bf16[4,40,8,128]{3,2,1,0:T(8,128)(2,1)S(1)} collective-permute-done((bf16[4,40,8,128]{3,2,1,0:T(8,128)(2,1)}, bf16[4,40,8,128]{3,2,1,0:T(8,128)(2,1)S(1)}, u32[]{:S(2)}, u32[]{:S(2)}) %collective-permute-start.4) | collective-permute-done | bytes 327712 | tf_op jit(solution)/shard_map/ppermute | solution.py:24
  53.2 1.2 %collective-permute-done.5.refs_4_ = bf16[4,40,8,128]{3,2,1,0:T(8,128)(2,1)S(1)} collective-permute-done((bf16[4,40,8,128]{3,2,1,0:T(8,128)(2,1)}, bf16[4,40,8,128]{3,2,1,0:T(8,128)(2,1)S(1)}, u32[]{:S(2)}, u32[]{:S(2)}) %collective-permute-start.5) | collective-permute-done | bytes 327712 | tf_op jit(solution)/shard_map/ppermute | solution.py:24
  54.5 0.0 copy-done.8
  54.5 0.0 copy-done.9
  54.5 0.9 %copy-done.5 = bf16[2,8,2688]{2,1,0:T(8,128)(2,1)S(1)} copy-done((bf16[2,8,2688]{2,1,0:T(8,128)(2,1)S(1)}, bf16[2,8,2688]{2,1,0:T(8,128)(2,1)}, u32[]{:S(2)}) %copy-start.5) | copy-done | bytes 86040
  55.4 1.0 %copy-done.7 = bf16[4,40,8,128]{3,2,1,0:T(8,128)(2,1)S(1)} copy-done((bf16[4,40,8,128]{3,2,1,0:T(8,128)(2,1)S(1)}, bf16[4,40,8,128]{3,2,1,0:T(8,128)(2,1)}, u32[]{:S(2)}) %copy-start.7) | copy-done | bytes 327704
  56.3 11.1 %shard_map.124 = (bf16[40,8,2688]{2,1,0:T(8,128)(2,1)}, bf16[2,8,2688]{2,1,0:T(8,128)(2,1)}) custom-call(s32[84]{0:T(128)S(1)} %reshape.59.depart_ref, s32[21,4,128]{2,1,0:T(4,128)S(1)} %copy-done.9, bf16[21,4,4,128]{3,2,1,0:T(4,128)(2,1)S(1)} %copy-done.8, bf16[2,8,2688]{2,1,0:T(8,128)(2,1)S(1)} %copy-done.5, ...), custom_call_target="tpu_custom_call" | custom-call | flops 880803840 | bytes 4000000 | tf_op jit(solution)/shard_map/pallas_call | solution.py:258
  (12 shorter events, 0.1 us)
Async XLA Ops:
  1.7 1.9 %copy-start.1 = (bf16[4,8,80,640]{3,2,1,0:T(8,128)(2,1)S(1)}, bf16[4,8,80,640]{3,2,1,0:T(8,128)(2,1)}, u32[]{:S(2)}) copy-start(bf16[4,8,80,640]{3,2,1,0:T(8,128)(2,1)} %param.10) | copy-start | bytes 9830404
  3.6 1.1 %copy-start.2 = (bf16[80,8,640]{2,1,0:T(8,128)(2,1)S(1)}, bf16[80,8,640]{2,1,0:T(8,128)(2,1)}, u32[]{:S(2)}) copy-start(bf16[80,8,640]{2,1,0:T(8,128)(2,1)} %val_ref.1) | copy-start | bytes 2457604
  4.7 1.1 %copy-start.3 = (bf16[80,8,640]{2,1,0:T(8,128)(2,1)S(1)}, bf16[80,8,640]{2,1,0:T(8,128)(2,1)}, u32[]{:S(2)}) copy-start(bf16[80,8,640]{2,1,0:T(8,128)(2,1)} %slope_ref.1) | copy-start | bytes 2457604
  5.9 10.0 %copy-start = (bf16[40,8,1,2688]{3,1,2,0:T(8,128)(2,1)S(1)}, bf16[40,8,1,2688]{3,1,2,0:T(8,128)(2,1)}, u32[]{:S(2)}) copy-start(bf16[40,8,1,2688]{3,1,2,0:T(8,128)(2,1)} %param.14) | copy-start | bytes 5160964
  10.2 13.3 %copy-start.10 = (s32[640]{0:T(1024)S(1)}, s32[640]{0:T(1024)}, u32[]{:S(2)}) copy-start(s32[640]{0:T(1024)} %param.13) | copy-start | bytes 7684
  10.2 13.4 %copy-start.11 = (s32[1,5,4]{1,2,0:T(4,128)S(1)}, s32[1,5,4]{1,2,0:T(4,128)}, u32[]{:S(2)}) copy-start(s32[1,5,4]{1,2,0:T(4,128)} %param.16) | copy-start | bytes 244
  10.2 18.7 %copy-start.4 = (bf16[3,8,1,2688]{3,1,2,0:T(8,128)(2,1)S(1)}, bf16[3,8,1,2688]{3,1,2,0:T(8,128)(2,1)}, u32[]{:S(2)}) copy-start(bf16[3,8,1,2688]{3,1,2,0:T(8,128)(2,1)} %param.15) | copy-start | bytes 387076
  10.2 33.4 %all-to-all-start = ((bf16[8,32,128]{2,1,0:T(8,128)(2,1)}), bf16[8,32,128]{2,1,0:T(8,128)(2,1)S(1)}, u32[]{:S(2)}, u32[]{:S(2)}) async-start(bf16[8,32,128]{2,1,0:T(8,128)(2,1)} %shard_map.121), calls=%async_computation | async-start | bytes 131072 | tf_op jit(solution)/shard_map/all_to_all | solution.py:306
  17.3 10.3 %collective-permute-start.1 = (bf16[40,1,2688]{2,1,0:T(2,128)(2,1)}, bf16[40,1,2688]{2,1,0:T(2,128)(2,1)S(1)}, u32[]{:S(2)}, u32[]{:S(2)}) collective-permute-start(bf16[40,1,2688]{2,1,0:T(2,128)(2,1)} %get-tuple-element.23), channel_id=1, source_target_pairs={{1,0},{2,1},{3,2},{5,4},{6,5},{7,6},{9,8},{10,9},{11,10},{13,12},{... | collective-permute-start | bytes 645128 | tf_op jit(solution)/shard_map/ppermute | solution.py:24
  20.4 8.5 %collective-permute-start = (bf16[40,1,2688]{2,1,0:T(2,128)(2,1)}, bf16[40,1,2688]{2,1,0:T(2,128)(2,1)S(1)}, u32[]{:S(2)}, u32[]{:S(2)}) collective-permute-start(bf16[40,1,2688]{2,1,0:T(2,128)(2,1)} %get-tuple-element.24), channel_id=1, source_target_pairs={{0,1},{1,2},{2,3},{4,5},{5,6},{6,7},{8,9},{9,10},{10,11},{12,13},{... | collective-permute-start | bytes 645128 | tf_op jit(solution)/shard_map/ppermute | solution.py:24
  26.4 17.0 %copy-start.12 = (s32[21,4]{0,1:T(4,128)S(1)}, s32[21,4]{0,1:T(4,128)}, u32[]{:S(2)}) copy-start(s32[21,4]{0,1:T(4,128)} %param.17) | copy-start | bytes 1012
  28.9 25.6 %copy-start.8 = (bf16[21,4,4,128]{3,2,1,0:T(4,128)(2,1)S(1)}, bf16[21,4,4,128]{3,2,1,0:T(4,128)(2,1)}, u32[]{:S(2)}) copy-start(bf16[21,4,4,128]{3,2,1,0:T(4,128)(2,1)} %weight_ref.1) | copy-start | bytes 258052
  28.9 25.6 %copy-start.9 = (s32[21,4,128]{2,1,0:T(4,128)S(1)}, s32[21,4,128]{2,1,0:T(4,128)}, u32[]{:S(2)}) copy-start(s32[21,4,128]{2,1,0:T(4,128)} %start_ref.1) | copy-start | bytes 129028
  31.8 0.7 %copy-start.6 = (bf16[4,40,8,128]{3,2,1,0:T(8,128)(2,1)}, bf16[4,40,8,128]{3,2,1,0:T(8,128)(2,1)S(1)}, u32[]{:S(2)}) copy-start(bf16[4,40,8,128]{3,2,1,0:T(8,128)(2,1)S(1)} %get-tuple-element.12.refs_2_) | copy-start | bytes 983044
  32.6 12.2 %collective-permute-start.2 = (bf16[4,40,8,128]{3,2,1,0:T(8,128)(2,1)}, bf16[4,40,8,128]{3,2,1,0:T(8,128)(2,1)S(1)}, u32[]{:S(2)}, u32[]{:S(2)}) collective-permute-start(bf16[4,40,8,128]{3,2,1,0:T(8,128)(2,1)} %get-tuple-element.10), channel_id=1, source_target_pairs={{8,0},{12,4},{16,8},{20,12},{24,16},{28,20},{9,1},{13,5},{17,9},{2... | collective-permute-start | bytes 983048 | tf_op jit(solution)/shard_map/ppermute | solution.py:24
  34.8 14.8 %collective-permute-start.3 = (bf16[4,40,8,128]{3,2,1,0:T(8,128)(2,1)}, bf16[4,40,8,128]{3,2,1,0:T(8,128)(2,1)S(1)}, u32[]{:S(2)}, u32[]{:S(2)}) collective-permute-start(bf16[4,40,8,128]{3,2,1,0:T(8,128)(2,1)} %get-tuple-element.11), channel_id=1, source_target_pairs={{4,0},{8,4},{12,8},{16,12},{20,16},{24,20},{28,24},{5,1},{9,5},{13... | collective-permute-start | bytes 983048 | tf_op jit(solution)/shard_map/ppermute | solution.py:24
  37.0 16.3 %collective-permute-start.4 = (bf16[4,40,8,128]{3,2,1,0:T(8,128)(2,1)}, bf16[4,40,8,128]{3,2,1,0:T(8,128)(2,1)S(1)}, u32[]{:S(2)}, u32[]{:S(2)}) collective-permute-start(bf16[4,40,8,128]{3,2,1,0:T(8,128)(2,1)} %get-tuple-element.13), channel_id=1, source_target_pairs={{0,4},{4,8},{8,12},{12,16},{16,20},{20,24},{24,28},{1,5},{5,9},{9,... | collective-permute-start | bytes 983048 | tf_op jit(solution)/shard_map/ppermute | solution.py:24
  41.0 13.5 %collective-permute-start.5 = (bf16[4,40,8,128]{3,2,1,0:T(8,128)(2,1)}, bf16[4,40,8,128]{3,2,1,0:T(8,128)(2,1)S(1)}, u32[]{:S(2)}, u32[]{:S(2)}) collective-permute-start(bf16[4,40,8,128]{3,2,1,0:T(8,128)(2,1)} %get-tuple-element.14), channel_id=1, source_target_pairs={{0,8},{4,12},{8,16},{12,20},{16,24},{20,28},{1,9},{5,13},{9,17},{1... | collective-permute-start | bytes 983048 | tf_op jit(solution)/shard_map/ppermute | solution.py:24
  54.5 0.9 %copy-start.5 = (bf16[2,8,2688]{2,1,0:T(8,128)(2,1)S(1)}, bf16[2,8,2688]{2,1,0:T(8,128)(2,1)}, u32[]{:S(2)}) copy-start(bf16[2,8,2688]{2,1,0:T(8,128)(2,1)} %shard_map.122.wind_ref) | copy-start | bytes 258052
  55.4 1.0 %copy-start.7 = (bf16[4,40,8,128]{3,2,1,0:T(8,128)(2,1)S(1)}, bf16[4,40,8,128]{3,2,1,0:T(8,128)(2,1)}, u32[]{:S(2)}) copy-start(bf16[4,40,8,128]{3,2,1,0:T(8,128)(2,1)} %copy-done.6) | copy-start | bytes 983044

commit v2 on v0

v2 whole, which is shorter than its diff:
```python
import functools
import math

import jax
import jax.numpy as jnp
from jax import lax
from jax.experimental import pallas as pl
from jax.experimental.pallas import tpu as pltpu
from jax.sharding import PartitionSpec as P

WAVES = 640
NLON = 2688
BLK = 128
GROUP = 16
LANES = 128
LIMIT = 48 * 2**20
VMEM = pl.BlockSpec(memory_space=pltpu.VMEM)
SMEM = pl.BlockSpec(memory_space=pltpu.SMEM)


ANY = pl.BlockSpec(memory_space=pl.ANY)
MESH = pl.DeviceIdType.MESH


def padded_to(value, axis, multiple):
    extra = -value.shape[axis] % multiple
    if extra == 0:
        return value
    widths = [(0, 0)] * value.ndim
    widths[axis] = (0, extra)
    return jnp.pad(value, widths)


def angle_tables(wave_numbers, shard_count, lanes, block_count):
    waves = padded_to(wave_numbers.reshape(shard_count, -1), 1, lanes).reshape(-1)
    scale = 2.0 * math.pi / NLON
    doubled = jnp.where(waves == 0, 1.0, 2.0).astype(jnp.float32)
    starts = jnp.arange(block_count, dtype=jnp.int32) * BLK
    coarse = (starts[:, None] * waves[None, :] % NLON).astype(jnp.float32) * scale
    fine = jnp.arange(BLK, dtype=jnp.int32)
    fine = (waves[:, None] * fine[None, :] % NLON).astype(jnp.float32) * scale
    table = jnp.concatenate([jnp.cos(fine), jnp.sin(fine)], axis=0).astype(jnp.bfloat16)
    return doubled * jnp.cos(coarse), doubled * jnp.sin(coarse), table


def block_of(index):
    return pl.ds(pl.multiple_of(index * BLK, BLK), BLK)


def gather_kernel(listed_ref, old_ref, weight_ref, blocks_ref, weights_ref):
    block_count = old_ref.shape[2] // BLK

    def take(slot, carry):
        lons = block_of(jnp.clip(listed_ref[slot], 0, block_count - 1))
        blocks_ref[slot] = old_ref[:, :, lons]
        weights_ref[slot] = weight_ref[:, :, lons]
        return carry

    lax.fori_loop(0, blocks_ref.shape[0], take, 0)


def listed_blocks(listed, old, weight):
    count = listed.shape[0]
    bins, k, _ = old.shape
    return pl.pallas_call(
        gather_kernel,
        out_shape=[
            jax.ShapeDtypeStruct((count, bins, k, BLK), jnp.bfloat16),
            jax.ShapeDtypeStruct((count, 3, k, BLK), jnp.bfloat16),
        ],
        in_specs=[SMEM, VMEM, VMEM],
        out_specs=[VMEM, VMEM],
        compiler_params=pltpu.CompilerParams(vmem_limit_bytes=LIMIT),
    )(listed, old, weight)


def arrive_kernel(depart_ref, stencil_ref, wind_ref, pool_ref, new_ref, flux_ref):
    bins, k, lon_count = new_ref.shape
    block_count, depth, _ = stencil_ref.shape
    stencil_rows = depth // BLK

    def arrive(c, carry):
        taken = [pool_ref[depart_ref[c * stencil_rows + t]] for t in range(stencil_rows)]
        new = jnp.dot(
            jnp.concatenate(taken, axis=1), stencil_ref[c], preferred_element_type=jnp.float32
        )
        new = new.astype(jnp.bfloat16).astype(jnp.float32).reshape(bins, k, BLK)
        lons = block_of(c)
        new_ref[:, :, lons] = new.astype(jnp.bfloat16)
        average = jnp.sum(new, axis=0) / bins
        wind = wind_ref[:, :, lons].astype(jnp.float32)
        flux_ref[:, :, lons] = (wind * average[None]).astype(jnp.bfloat16)
        return carry

    lax.fori_loop(0, block_count, arrive, 0)


def arrivals(depart_slot, stencil, wind, pool, bins):
    _, k, lon_count = wind.shape
    return pl.pallas_call(
        arrive_kernel,
        out_shape=[
            jax.ShapeDtypeStruct((bins, k, lon_count), jnp.bfloat16),
            jax.ShapeDtypeStruct((2, k, lon_count), jnp.bfloat16),
        ],
        in_specs=[SMEM] + [VMEM] * 3,
        out_specs=[VMEM, VMEM],
        compiler_params=pltpu.CompilerParams(vmem_limit_bytes=LIMIT),
        cost_estimate=pl.CostEstimate(
            flops=2 * stencil.size * bins * k, bytes_accessed=4_000_000, transcendentals=0
        ),
    )(depart_slot.reshape(-1), stencil, wind, pool)


def step_kernel(
    sizes,
    spec_ref,
    val_ref,
    slope_ref,
    factor_ref,
    old_ref,
    weight_ref,
    cos_ref,
    sin_ref,
    table_ref,
    start_ref,
    points_ref,
    wind_ref,
    pool,
    stencil,
    spec,
    val,
    slope,
    old,
    low,
    high,
    below,
    above,
    outgoing,
    acc,
    terms_out,
    terms_in,
    lhs,
    grid,
    load_sem,
    halo_send,
    halo_recv,
    term_send,
    term_recv,
    block_send,
    block_recv,
):
    bands, levs, offsets, slots = sizes
    band, lev = lax.axis_index("band"), lax.axis_index("lev")
    _, bins, k, _ = old.shape
    block_count = wind_ref.shape[2] // BLK
    rows = bins * k
    reach = offsets // 2

    loads = [
        pltpu.make_async_copy(source, target, load_sem.at[i])
        for i, (source, target) in enumerate(
            [(old_ref, old), (spec_ref, spec), (val_ref, val), (slope_ref, slope)]
        )
    ]
    for load in loads:
        load.start()

    barrier = pltpu.get_barrier_semaphore()
    for d in range(1, bands):
        peer = lax.rem(band + d, bands)
        pl.semaphore_signal(barrier, inc=1, device_id={"band": peer}, device_id_type=MESH)
    after = lax.rem(lev + 1, levs)
    before = lax.rem(lev + levs - 1, levs)

    for beside in (after, before):
        pl.semaphore_signal(barrier, inc=1, device_id={"lev": beside}, device_id_type=MESH)

    loads[0].wait()

    def edges(slot, carry):
        whole = old[slot].astype(jnp.float32)
        low[slot] = whole[:, 0, :].astype(jnp.bfloat16)
        high[slot] = whole[:, k - 1, :].astype(jnp.bfloat16)
        return carry

    lax.fori_loop(0, offsets * slots, edges, 0)

    @pl.when(lev == 0)
    def _():
        below[...] = jnp.zeros_like(below)

    @pl.when(lev == levs - 1)
    def _():
        above[...] = jnp.zeros_like(above)

    pl.semaphore_wait(barrier, bands + 1)

    up = pltpu.make_async_remote_copy(
        src_ref=high,
        dst_ref=below,
        send_sem=halo_send.at[0],
        recv_sem=halo_recv.at[0],
        device_id={"lev": after},
        device_id_type=MESH,
    )
    down = pltpu.make_async_remote_copy(
        src_ref=low,
        dst_ref=above,
        send_sem=halo_send.at[1],
        recv_sem=halo_recv.at[1],
        device_id={"lev": before},
        device_id_type=MESH,
    )

    @pl.when(lev < levs - 1)
    def _():
        up.start()

    @pl.when(lev > 0)
    def _():
        down.start()

    stencil_rows = start_ref.shape[1]
    points = points_ref.shape[2]
    q = lax.broadcasted_iota(jnp.int32, (BLK, BLK), 0)

    def build(c, carry):
        starts = start_ref[c]
        for t in range(stencil_rows):
            away = q - starts[t : t + 1, :]
            weights = points_ref[c, t].astype(jnp.float32)
            matrix = jnp.zeros((BLK, BLK), jnp.float32)
            for u in range(points):
                matrix = jnp.where(away == u, weights[u : u + 1, :], matrix)
            stencil[c, t * BLK : (t + 1) * BLK, :] = matrix.astype(jnp.bfloat16)
        return carry

    lax.fori_loop(0, block_count, build, 0)

    @pl.when(lev > 0)
    def _():
        up.wait_recv()

    @pl.when(lev < levs - 1)
    def _():
        down.wait_recv()

    level = lax.broadcasted_iota(jnp.int32, (1, k, BLK), 1)

    def remapped(slot):
        weights = weight_ref[slot].astype(jnp.float32)
        here = old[slot].astype(jnp.float32)
        under = below[slot].astype(jnp.float32)[:, None, :]
        over = above[slot].astype(jnp.float32)[:, None, :]
        lower = jnp.where(level == 0, under, pltpu.roll(here, 1, 1))
        upper = jnp.where(level == k - 1, over, pltpu.roll(here, k - 1, 1))
        summed = weights[0:1] * lower + weights[1:2] * here + weights[2:3] * upper
        return summed.reshape(rows, BLK).astype(jnp.bfloat16)

    copies = []
    for o in sorted(range(offsets), key=lambda o: (-abs(o - reach), o)):

        def fill(e, carry, o=o):
            outgoing[o * slots + e] = remapped(o * slots + e)
            return carry

        lax.fori_loop(0, slots, fill, 0)
        at = pl.ds(o * slots, slots)
        if o == reach:
            kept = pltpu.make_async_copy(outgoing.at[at], pool.at[at], load_sem.at[4])
            kept.start()
            continue
        to, source = band + (o - reach), band - (o - reach)
        copy = pltpu.make_async_remote_copy(
            src_ref=outgoing.at[at],
            dst_ref=pool.at[at],
            send_sem=block_send.at[o],
            recv_sem=block_recv.at[o],
            device_id={"band": lax.rem(to + bands, bands)},
            device_id_type=MESH,
        )
        sends = (to >= 0) & (to < bands)
        receives = (source >= 0) & (source < bands)
        copies.append((copy, sends, receives))

        @pl.when(sends)
        def _(copy=copy):
            copy.start()

    for load in loads[1:]:
        load.wait()
    fields = spec.shape[0]
    lat_count = val.shape[1]
    trunc = spec.shape[2]
    cols = GROUP * lat_count
    width = acc.shape[1]
    lanes = width // lat_count
    own = lax.broadcasted_iota(jnp.int32, (GROUP, cols), 0)
    col = lax.broadcasted_iota(jnp.int32, (GROUP, cols), 1)
    keep = (col // lat_count == own)[None]
    row = lax.broadcasted_iota(jnp.int32, (cols, width), 0)
    lane = lax.broadcasted_iota(jnp.int32, (cols, width), 1)
    acc[...] = jnp.zeros_like(acc)

    def transform(g, carry):
        at = pl.ds(pl.multiple_of(g * GROUP, GROUP), GROUP)
        left = spec[:, at, :].reshape(fields * GROUP, trunc)

        def terms(table):
            right = table[at].reshape(cols, trunc)
            product = lax.dot_general(
                left, right, (((1,), (1,)), ((), ())), preferred_element_type=jnp.float32
            ).reshape(fields, GROUP, cols)
            return jnp.sum(jnp.where(keep, product, 0.0), axis=1)

        value, tilt = terms(val), terms(slope)
        factor = factor_ref[g]
        v = [value[x * k : (x + 1) * k] for x in range(4)]
        d = [tilt[x * k : (x + 1) * k] for x in range(4)]
        coefficients = jnp.concatenate(
            [
                -d[0] - factor * v[3],
                -d[1] + factor * v[2],
                d[2] - factor * v[1],
                d[3] + factor * v[0],
            ],
            axis=0,
        ).astype(jnp.bfloat16)
        slot = lane % lanes - g * GROUP
        hot = (slot * lat_count + lane // lanes == row) & (slot >= 0) & (slot < GROUP)
        hot = hot.astype(jnp.float32).astype(jnp.bfloat16)
        acc[...] += jnp.dot(coefficients, hot, preferred_element_type=jnp.float32)
        return carry

    lax.fori_loop(0, spec.shape[1] // GROUP, transform, 0)
    for lat in range(lat_count):
        terms_out[lat] = acc[:, lat * lanes : (lat + 1) * lanes].astype(jnp.bfloat16)
    exchanges = []
    for d in range(1, bands):
        peer = lax.rem(band + d, bands)
        copy = pltpu.make_async_remote_copy(
            src_ref=terms_out.at[peer],
            dst_ref=terms_in.at[band],
            send_sem=term_send.at[d],
            recv_sem=term_recv.at[d],
            device_id={"band": peer},
            device_id_type=MESH,
        )
        copy.start()
        exchanges.append(copy)
    terms_in[band] = terms_out[band]
    for copy in exchanges:
        copy.wait()

    whole = jnp.concatenate([terms_in[b] for b in range(bands)], axis=1).astype(jnp.float32)
    real = jnp.concatenate([whole[0:k], whole[2 * k : 3 * k]], axis=0)
    imag = jnp.concatenate([whole[k : 2 * k], whole[3 * k : 4 * k]], axis=0)
    span = whole.shape[1]

    def turn(c, carry):
        cos_c = cos_ref[pl.ds(c, 1), :]
        sin_c = sin_ref[pl.ds(c, 1), :]
        at = pl.ds(pl.multiple_of(c * 2 * k, 2 * k), 2 * k)
        lhs[at, 0:span] = (real * cos_c - imag * sin_c).astype(jnp.bfloat16)
        lhs[at, span : 2 * span] = (-real * sin_c - imag * cos_c).astype(jnp.bfloat16)
        return carry

    lax.fori_loop(0, block_count, turn, 0)
    grid[...] = jnp.dot(lhs[...], table_ref[...], preferred_element_type=jnp.float32)
    for c in range(block_count):
        for w in range(2):
            start = (2 * c + w) * k
            wind_ref[w, :, c * BLK : (c + 1) * BLK] = grid[start : start + k].astype(jnp.bfloat16)

    kept.wait()
    for copy, sends, receives in copies:

        @pl.when(receives)
        def _(copy=copy):
            copy.wait_recv()

    for copy, sends, receives in copies:

        @pl.when(sends)
        def _(copy=copy):
            copy.wait_send()

    @pl.when(lev < levs - 1)
    def _():
        up.wait_send()

    @pl.when(lev > 0)
    def _():
        down.wait_send()


def shards(
    spectral,
    legendre_value,
    legendre_slope,
    wave_numbers,
    aerosol_old,
    vertical_weight,
    send_blocks,
    depart_slot,
    depart_offset,
    depart_weight,
):
    band_here = lax.axis_index("band")
    bands, levs = lax.axis_size("band"), lax.axis_size("lev")
    fields, k, wave_local, trunc = spectral.shape
    bins, _, lat_here, lon_count = aerosol_old.shape
    lat_count = legendre_value.shape[1]
    block_count = lon_count // BLK
    offsets, slots = send_blocks.shape[1:]
    rows = fields * k
    old = aerosol_old.reshape(bins, k, lon_count)
    weight = vertical_weight.reshape(3, k, lon_count)

    own_waves = lax.dynamic_slice_in_dim(wave_numbers, band_here * wave_local, wave_local, 0)
    spec = padded_to(spectral.reshape(rows, wave_local, trunc), 1, GROUP)
    value = padded_to(legendre_value, 0, GROUP)
    slope = padded_to(legendre_slope, 0, GROUP)
    steps = spec.shape[1] // GROUP
    lanes = -(-spec.shape[1] // LANES) * LANES
    factor = padded_to(own_waves.astype(jnp.float32) / WAVES, 0, GROUP)
    factor = jnp.broadcast_to(factor[:, None], (factor.shape[0], lat_count))
    factor = factor.reshape(steps, 1, GROUP * lat_count)
    cos_block, sin_block, table = angle_tables(wave_numbers, bands, lanes, block_count)

    edge = pltpu.VMEM((offsets * slots, bins, BLK), jnp.bfloat16)
    blocks = pltpu.VMEM((offsets * slots, bins * k, BLK), jnp.bfloat16)
    terms = pltpu.VMEM((bands, rows, lanes), jnp.bfloat16)
    dma = pltpu.SemaphoreType.DMA
    listed, listed_weight = listed_blocks(send_blocks.reshape(-1), old, weight)
    wind, pool, stencil = pl.pallas_call(
        functools.partial(step_kernel, (bands, levs, offsets, slots)),
        out_shape=[
            jax.ShapeDtypeStruct((2, k, lon_count), jnp.bfloat16),
            jax.ShapeDtypeStruct((offsets * slots, bins * k, BLK), jnp.bfloat16),
            jax.ShapeDtypeStruct((block_count, depart_slot.shape[1] * BLK, BLK), jnp.bfloat16),
        ],
        in_specs=[ANY, ANY, ANY, VMEM, ANY] + [VMEM] * 6,
        out_specs=[VMEM, ANY, VMEM],
        scratch_shapes=[
            pltpu.VMEM(spec.shape, jnp.bfloat16),
            pltpu.VMEM(value.shape, jnp.bfloat16),
            pltpu.VMEM(slope.shape, jnp.bfloat16),
            pltpu.VMEM(listed.shape, jnp.bfloat16),
            edge,
            edge,
            edge,
            edge,
            blocks,
            pltpu.VMEM((rows, lat_count * lanes), jnp.float32),
            terms,
            terms,
            pltpu.VMEM((block_count * 2 * k, table.shape[0]), jnp.bfloat16),
            pltpu.VMEM((block_count * 2 * k, BLK), jnp.float32),
            dma((5,)),
            dma((2,)),
            dma((2,)),
            dma((bands,)),
            dma((bands,)),
            dma((offsets,)),
            dma((offsets,)),
        ],
        compiler_params=pltpu.CompilerParams(
            collective_id=0, has_side_effects=True, vmem_limit_bytes=LIMIT
        ),
        cost_estimate=pl.CostEstimate(
            flops=4_000_000_000, bytes_accessed=10_000_000, transcendentals=0
        ),
    )(
        spec,
        value,
        slope,
        factor,
        listed,
        listed_weight,
        cos_block,
        sin_block,
        table,
        depart_offset,
        depart_weight,
    )
    new, flux = arrivals(depart_slot, stencil, wind, pool, bins)
    lat_shape = (k, lat_here, lon_count)
    return (
        wind.reshape((2, *lat_shape)),
        new.reshape((bins, *lat_shape)),
        flux.reshape((2, *lat_shape)),
    )


def solution(mesh):
    return jax.shard_map(
        shards,
        mesh=mesh,
        in_specs=(
            P(None, "lev", "band", None),
            P("band", None, None),
            P("band", None, None),
            P(),
            P(None, "lev", "band", None),
            P(None, "lev", "band", None),
            P("band", None, None),
            P("band", None),
            P("band", None, None),
            P("band", None, None, None),
        ),
        out_specs=(
            P(None, "lev", "band", None),
            P(None, "lev", "band", None),
            P(None, "lev", "band", None),
        ),
        check_vma=False,
    )
```

time: 117 us -> 45.4 us (0.39)
  the two profiles are of different devices: /device:TPU:18 before, /device:TPU:1 now
where the time goes in v2:
time: 45.4 us; the launch traced here: 45.1 us
  Pallas kernels  36.3 us (80%)
  local copies, waits for them, and re-layouts  4.01 us (9%)
  other arithmetic  3.98 us (9%)
  between operations  0.8 us (2%)
    pallas_call x1, Pallas kernels, shards(): pl.pallas_call(functools.partial(step_kernel, (bands, levs, offsets, slot...  28.2 us
    pallas_call x1, Pallas kernels, arrivals(): pl.pallas_call(arrive_kernel, out_shape=[jax.ShapeDtypeStruct((bins, k, l...  7.05 us
    unnamed x21, local copies, waits for them, and re-layouts  2.69 us
    another operation x1, other arithmetic  2.61 us
    pallas_call x1, Pallas kernels, listed_blocks(): pl.pallas_call(gather_kernel, out_shape=[jax.ShapeDtypeStruct((count, bin...  1.05 us

profile of v2, /device:TPU:1, one launch (start us, length us, event | category | flops | bytes accessed | tf_op | source)
XLA Modules:
  0.0 45.1 jit_solution(5002271155020473502)
XLA Ops:
  0.6 0.0 copy-start.7
  0.6 0.0 copy-start.1
  0.7 0.0 copy-start.2
  0.7 0.9 %reshape.62 = s32[8,80]{1,0:T(8,128)S(1)} reshape(s32[640]{0:T(1024)} %param.13) | data formatting | bytes 5120 | tf_op jit(solution)/shard_map/reshape | solution.py:35
  1.6 2.6 %cosine_convert_fusion = (bf16[1024,128]{1,0:T(8,128)(2,1)S(1)}, bf16[1024,128]{1,0:T(8,128)(2,1)S(1)}) fusion(s32[1024]{0:T(1024)S(1)} %pad_bitcast_fusion), kind=kLoop, calls=%fused_computation.5 | loop fusion | flops 1441792 | bytes 528384 | tf_op jit(solution)/shard_map/convert
  4.2 0.0 copy-start.3
  4.2 0.0 copy-start.5
  4.2 0.0 copy-start.6
  4.3 0.8 %convert_multiply_fusion = f32[80]{0:T(128)S(1)} fusion(s32[640]{0:T(1024)} %param.13, s32[]{:T(128)S(6)} %select_n.24), kind=kLoop, calls=%fused_computation.22 | loop fusion | flops 160 | bytes 644 | tf_op jit(solution)/shard_map/div | solution.py:427
  5.1 0.1 broadcast_in_dim.22
  5.2 0.1 broadcast_in_dim.23
  5.2 0.1 broadcast_in_dim.27.factor_ref
  5.4 0.5 %sine_multiply_fusion = (f32[21,1024]{1,0:T(8,128)S(1)}, f32[21,1024]{1,0:T(8,128)S(1)}) fusion(s32[1024]{0:T(1024)S(1)} %pad_bitcast_fusion, s32[21]{0:T(128)S(1)} %iota_multiply_fusion, f32[1024]{0:T(1024)S(1)} %compare_select_fusion), kind=kLoop, calls=%fused_computation.13 | loop fusion | flops 236544 | bytes 180308 | tf_op jit(solution)/shard_map/mul | solution.py:43
  5.9 0.0 copy-done.7
  5.9 0.1 copy.18
  6.0 0.1 reshape.59.listed_ref
  6.1 0.0 copy-start.4
  6.1 0.0 copy-done.1
  6.1 0.0 copy-done.2
  6.1 1.0 %shard_map.121 = (bf16[20,40,8,128]{3,2,1,0:T(8,128)(2,1)S(1)}, bf16[20,3,8,128]{3,2,1,0:T(8,128)(2,1)S(1)}) custom-call(s32[20]{0:T(128)S(1)} %reshape.59.listed_ref, bf16[40,8,2688]{2,1,0:T(8,128)(2,1)S(1)} %bitcast.16, bf16[3,8,2688]{2,1,0:T(8,128)(2,1)S(1)} %bitcast.18), custom_call_target="tpu_custom_call" | custom-call | tf_op jit(solution)/shard_map/pallas_call | solution.py:65
  7.1 0.0 copy-done.3
  7.1 0.0 copy-done.5
  7.1 0.0 copy-done.6
  7.2 0.1 copy-done.4
  7.2 0.0 copy-start.8
  7.2 28.2 %shard_map.122 = (bf16[2,8,2688]{2,1,0:T(8,128)(2,1)S(1)}, bf16[20,320,128]{2,1,0:T(8,128)(2,1)S(1)}, bf16[21,512,128]{2,1,0:T(8,128)(2,1)}) custom-call(bf16[32,80,640]{2,1,0:T(8,128)(2,1)} %bitcast.19, bf16[80,8,640]{2,1,0:T(8,128)(2,1)S(1)} %copy-done.3, bf16[80,8,640]{2,1,0:T(8,128)(2,1)S(1)} %copy-done.4, f32[5,1,128]{2,1,0:T(1,128)S(1)} %broadcast_in_dim.27.factor_ref, ...), custom_call_target="tpu_custom_call" | custom-call | flops 4000000000 | bytes 10000000 | tf_op jit(solution)/shard_map/pallas_call | solution.py:437
  35.5 0.0 copy-done.8
  35.5 0.1 copy.20
  35.6 0.1 reshape.65.depart_ref
  35.7 0.0 copy-start
  35.7 1.8 %copy-done = bf16[21,512,128]{2,1,0:T(8,128)(2,1)S(1)} copy-done((bf16[21,512,128]{2,1,0:T(8,128)(2,1)S(1)}, bf16[21,512,128]{2,1,0:T(8,128)(2,1)}, u32[]{:S(2)}) %copy-start) | copy-done | bytes 2752536
  37.4 7.0 %shard_map.123 = (bf16[40,8,2688]{2,1,0:T(8,128)(2,1)}, bf16[2,8,2688]{2,1,0:T(8,128)(2,1)}) custom-call(s32[84]{0:T(128)S(1)} %reshape.65.depart_ref, bf16[21,512,128]{2,1,0:T(8,128)(2,1)S(1)} %copy-done, bf16[2,8,2688]{2,1,0:T(8,128)(2,1)S(1)} %get-tuple-element.12.wind_ref, bf16[20,320,128]{2,1,0:T(8,128)(2,1)S(1)} %get-tuple-element.14.pool_ref), custom_call_target="tpu_custom_call" | custom-call | flops 880803840 | bytes 4000000 | tf_op jit(solution)/shard_map/pallas_call | solution.py:100
  44.5 0.6 %copy.25 = bf16[2,8,1,2688]{3,1,2,0:T(8,128)(2,1)} copy(bf16[2,8,1,2688]{3,1,2,0:T(8,128)(2,1)S(1)} %bitcast.17) | data formatting | bytes 172032
  (4 shorter events, 0.1 us)
Async XLA Ops:
  0.6 5.2 %copy-start.7 = (s32[1,5,4]{1,2,0:T(4,128)S(1)}, s32[1,5,4]{1,2,0:T(4,128)}, u32[]{:S(2)}) copy-start(s32[1,5,4]{1,2,0:T(4,128)} %param.16) | copy-start | bytes 244
  0.6 5.4 %copy-start.1 = (bf16[40,8,1,2688]{3,1,2,0:T(8,128)(2,1)S(1)}, bf16[40,8,1,2688]{3,1,2,0:T(8,128)(2,1)}, u32[]{:S(2)}) copy-start(bf16[40,8,1,2688]{3,1,2,0:T(8,128)(2,1)} %param.14) | copy-start | bytes 5160964
  0.7 5.4 %copy-start.2 = (bf16[3,8,1,2688]{3,1,2,0:T(8,128)(2,1)S(1)}, bf16[3,8,1,2688]{3,1,2,0:T(8,128)(2,1)}, u32[]{:S(2)}) copy-start(bf16[3,8,1,2688]{3,1,2,0:T(8,128)(2,1)} %param.15) | copy-start | bytes 387076
  4.2 2.9 %copy-start.3 = (bf16[80,8,640]{2,1,0:T(8,128)(2,1)S(1)}, bf16[80,8,640]{2,1,0:T(8,128)(2,1)}, u32[]{:S(2)}) copy-start(bf16[80,8,640]{2,1,0:T(8,128)(2,1)} %val_ref.1) | copy-start | bytes 2457604
  4.2 2.9 %copy-start.5 = (bf16[21,4,4,128]{3,2,1,0:T(4,128)(2,1)S(1)}, bf16[21,4,4,128]{3,2,1,0:T(4,128)(2,1)}, u32[]{:S(2)}) copy-start(bf16[21,4,4,128]{3,2,1,0:T(4,128)(2,1)} %points_ref.1) | copy-start | bytes 258052
  4.2 2.9 %copy-start.6 = (s32[21,4,128]{2,1,0:T(4,128)S(1)}, s32[21,4,128]{2,1,0:T(4,128)}, u32[]{:S(2)}) copy-start(s32[21,4,128]{2,1,0:T(4,128)} %start_ref.1) | copy-start | bytes 129028
  6.1 1.1 %copy-start.4 = (bf16[80,8,640]{2,1,0:T(8,128)(2,1)S(1)}, bf16[80,8,640]{2,1,0:T(8,128)(2,1)}, u32[]{:S(2)}) copy-start(bf16[80,8,640]{2,1,0:T(8,128)(2,1)} %slope_ref.1) | copy-start | bytes 2457604
  7.2 28.3 %copy-start.8 = (s32[21,4]{0,1:T(4,128)S(1)}, s32[21,4]{0,1:T(4,128)}, u32[]{:S(2)}) copy-start(s32[21,4]{0,1:T(4,128)} %param.17) | copy-start | bytes 1012
  35.7 1.8 %copy-start = (bf16[21,512,128]{2,1,0:T(8,128)(2,1)S(1)}, bf16[21,512,128]{2,1,0:T(8,128)(2,1)}, u32[]{:S(2)}) copy-start(bf16[21,512,128]{2,1,0:T(8,128)(2,1)} %get-tuple-element.13.stencil_ref) | copy-start | bytes 8257540

commit v3 on v2

--- a/solution.py
+++ b/solution.py
@@ -13,7 +13,8 @@
 BLK = 128
 GROUP = 16
 LANES = 128
-LIMIT = 48 * 2**20
+FINE = 16
+LIMIT = 16 * 2**20
 VMEM = pl.BlockSpec(memory_space=pltpu.VMEM)
 SMEM = pl.BlockSpec(memory_space=pltpu.SMEM)
 
@@ -29,18 +30,6 @@
     widths = [(0, 0)] * value.ndim
     widths[axis] = (0, extra)
     return jnp.pad(value, widths)
-
-
-def angle_tables(wave_numbers, shard_count, lanes, block_count):
-    waves = padded_to(wave_numbers.reshape(shard_count, -1), 1, lanes).reshape(-1)
-    scale = 2.0 * math.pi / NLON
-    doubled = jnp.where(waves == 0, 1.0, 2.0).astype(jnp.float32)
-    starts = jnp.arange(block_count, dtype=jnp.int32) * BLK
-    coarse = (starts[:, None] * waves[None, :] % NLON).astype(jnp.float32) * scale
-    fine = jnp.arange(BLK, dtype=jnp.int32)
-    fine = (waves[:, None] * fine[None, :] % NLON).astype(jnp.float32) * scale
-    table = jnp.concatenate([jnp.cos(fine), jnp.sin(fine)], axis=0).astype(jnp.bfloat16)
-    return doubled * jnp.cos(coarse), doubled * jnp.sin(coarse), table
 
 
 def block_of(index):
@@ -120,9 +109,7 @@
     factor_ref,
     old_ref,
     weight_ref,
-    cos_ref,
-    sin_ref,
-    table_ref,
+    waves_ref,
     start_ref,
     points_ref,
     wind_ref,
@@ -142,6 +129,9 @@
     terms_in,
     lhs,
     grid,
+    cos_ref,
+    sin_ref,
+    table,
     load_sem,
     halo_send,
     halo_recv,
@@ -301,6 +291,7 @@
     keep = (col // lat_count == own)[None]
     row = lax.broadcasted_iota(jnp.int32, (cols, width), 0)
     lane = lax.broadcasted_iota(jnp.int32, (cols, width), 1)
+    place = lane % lanes * lat_count + lane // lanes - row
     acc[...] = jnp.zeros_like(acc)
 
     def transform(g, carry):
@@ -327,9 +318,7 @@
             ],
             axis=0,
         ).astype(jnp.bfloat16)
-        slot = lane % lanes - g * GROUP
-        hot = (slot * lat_count + lane // lanes == row) & (slot >= 0) & (slot < GROUP)
-        hot = hot.astype(jnp.float32).astype(jnp.bfloat16)
+        hot = (place == g * cols).astype(jnp.float32).astype(jnp.bfloat16)
         acc[...] += jnp.dot(coefficients, hot, preferred_element_type=jnp.float32)
         return carry
 
@@ -350,13 +339,32 @@
         copy.start()
         exchanges.append(copy)
     terms_in[band] = terms_out[band]
+
+    waves = waves_ref[...]
+    span = waves.shape[1]
+
+    def angles(count, stride):
+        turns = lax.broadcasted_iota(jnp.int32, (count, span), 0) * stride
+        turns = lax.rem(turns * waves, NLON).astype(jnp.float32) * (2.0 * math.pi / NLON)
+        return jnp.cos(turns), jnp.sin(turns)
+
+    doubled = jnp.where(waves == 0, 1.0, 2.0)
+    cos_c, sin_c = angles(cos_ref.shape[0], BLK)
+    cos_ref[...] = doubled * cos_c
+    sin_ref[...] = doubled * sin_c
+    cos_a, sin_a = angles(BLK // FINE, FINE)
+    cos_b, sin_b = angles(FINE, 1)
+    for a in range(BLK // FINE):
+        ca, sa = cos_a[a : a + 1], sin_a[a : a + 1]
+        at = slice(a * FINE, (a + 1) * FINE)
+        table[at, 0:span] = (ca * cos_b - sa * sin_b).astype(jnp.bfloat16)
+        table[at, span : 2 * span] = (sa * cos_b + ca * sin_b).astype(jnp.bfloat16)
     for copy in exchanges:
         copy.wait()
 
     whole = jnp.concatenate([terms_in[b] for b in range(bands)], axis=1).astype(jnp.float32)
     real = jnp.concatenate([whole[0:k], whole[2 * k : 3 * k]], axis=0)
     imag = jnp.concatenate([whole[k : 2 * k], whole[3 * k : 4 * k]], axis=0)
-    span = whole.shape[1]
 
     def turn(c, carry):
         cos_c = cos_ref[pl.ds(c, 1), :]
@@ -367,7 +375,9 @@
         return carry
 
     lax.fori_loop(0, block_count, turn, 0)
-    grid[...] = jnp.dot(lhs[...], table_ref[...], preferred_element_type=jnp.float32)
+    grid[...] = lax.dot_general(
+        lhs[...], table[...], (((1,), (1,)), ((), ())), preferred_element_type=jnp.float32
+    )
     for c in range(block_count):
         for w in range(2):
             start = (2 * c + w) * k
@@ -427,7 +437,9 @@
     factor = padded_to(own_waves.astype(jnp.float32) / WAVES, 0, GROUP)
     factor = jnp.broadcast_to(factor[:, None], (factor.shape[0], lat_count))
     factor = factor.reshape(steps, 1, GROUP * lat_count)
-    cos_block, sin_block, table = angle_tables(wave_numbers, bands, lanes, block_count)
+    waves = padded_to(wave_numbers.reshape(bands, wave_local), 1, lanes).reshape(1, -1)
+    span = bands * lanes
+    coarse = pltpu.VMEM((-(-block_count // 8) * 8, span), jnp.float32)
 
     edge = pltpu.VMEM((offsets * slots, bins, BLK), jnp.bfloat16)
     blocks = pltpu.VMEM((offsets * slots, bins * k, BLK), jnp.bfloat16)
@@ -441,7 +453,7 @@
             jax.ShapeDtypeStruct((offsets * slots, bins * k, BLK), jnp.bfloat16),
             jax.ShapeDtypeStruct((block_count, depart_slot.shape[1] * BLK, BLK), jnp.bfloat16),
         ],
-        in_specs=[ANY, ANY, ANY, VMEM, ANY] + [VMEM] * 6,
+        in_specs=[ANY, ANY, ANY, VMEM, ANY] + [VMEM] * 4,
         out_specs=[VMEM, ANY, VMEM],
         scratch_shapes=[
             pltpu.VMEM(spec.shape, jnp.bfloat16),
@@ -456,8 +468,11 @@
             pltpu.VMEM((rows, lat_count * lanes), jnp.float32),
             terms,
             terms,
-            pltpu.VMEM((block_count * 2 * k, table.shape[0]), jnp.bfloat16),
+            pltpu.VMEM((block_count * 2 * k, 2 * span), jnp.bfloat16),
             pltpu.VMEM((block_count * 2 * k, BLK), jnp.float32),
+            coarse,
+            coarse,
+            pltpu.VMEM((BLK, 2 * span), jnp.bfloat16),
             dma((5,)),
             dma((2,)),
             dma((2,)),
@@ -467,7 +482,7 @@
             dma((offsets,)),
         ],
         compiler_params=pltpu.CompilerParams(
-            collective_id=0, has_side_effects=True, vmem_limit_bytes=LIMIT
+            collective_id=0, has_side_effects=True, vmem_limit_bytes=(44 + bands // 8) * 2**20
         ),
         cost_estimate=pl.CostEstimate(
             flops=4_000_000_000, bytes_accessed=10_000_000, transcendentals=0
@@ -479,9 +494,7 @@
         factor,
         listed,
         listed_weight,
-        cos_block,
-        sin_block,
-        table,
+        waves,
         depart_offset,
         depart_weight,
     )

time: 45.4 us -> 42.6 us (0.938)
  other arithmetic: 3.98 us -> 0.8 us
  local copies, waits for them, and re-layouts: 4.01 us -> 6.05 us
  Pallas kernels: 36.3 us -> 34.8 us
    another operation x1 -> x0, other arithmetic: 2.61 us -> none
    unnamed x21 -> x15, local copies, waits for them, and re-layouts: 2.69 us -> 4.86 us
    pallas_call x1, Pallas kernels: 28.2 us -> 26.7 us  [shards(): pl.pallas_call(functools.partial(step_kernel, (bands, levs, offsets, slot...]
    mul x2 -> x0, other arithmetic: 0.5 us -> none  [the longest x1 0.49 us: angle_tables(): return (doubled * jnp.cos(coarse), doubled * jnp.sin(coarse), table)]
where the time goes in v3:
time: 42.6 us; the launch traced here: 42.3 us
  Pallas kernels  34.8 us (82%)
  local copies, waits for them, and re-layouts  6.05 us (14%)
  other arithmetic  0.8 us (2%)
  between operations  0.71 us (2%)
    pallas_call x1, Pallas kernels, shards(): pl.pallas_call(functools.partial(step_kernel, (bands, levs, offsets, slot...  26.7 us
    pallas_call x1, Pallas kernels, arrivals(): pl.pallas_call(arrive_kernel, out_shape=[jax.ShapeDtypeStruct((bins, k, l...  7.04 us
    unnamed x15, local copies, waits for them, and re-layouts  4.86 us
    pallas_call x1, Pallas kernels, listed_blocks(): pl.pallas_call(gather_kernel, out_shape=[jax.ShapeDtypeStruct((count, bin...  1.05 us

profile of v3, /device:TPU:1, one launch (start us, length us, event | category | flops | bytes accessed | tf_op | source)
XLA Modules:
  0.0 42.3 jit_solution(13860785095200462326)
XLA Ops:
  0.6 0.0 copy-start.4
  0.6 0.0 copy-start.5
  0.7 0.8 %convert_multiply_fusion = f32[80]{0:T(128)S(1)} fusion(s32[640]{0:T(1024)} %param.13, s32[]{:T(128)S(6)} %select_n.3), kind=kLoop, calls=%fused_computation | loop fusion | flops 160 | bytes 644 | tf_op jit(solution)/shard_map/div | solution.py:437
  1.5 0.1 broadcast_in_dim.10
  1.5 0.8 %copy.18 = s32[1,5,4]{2,1,0:T(8,128)S(1)} copy(s32[1,5,4]{1,2,0:T(4,128)} %param.16) | data formatting | bytes 160 | tf_op args[6]
  2.3 0.1 reshape.47.listed_ref
  2.4 0.8 %reshape.50 = s32[8,80]{1,0:T(8,128)S(1)} reshape(s32[640]{0:T(1024)} %param.13) | data formatting | bytes 5120 | tf_op jit(solution)/shard_map/reshape | solution.py:440
  3.2 0.8 %copy.20 = s32[21,4]{1,0:T(8,128)S(1)} copy(s32[21,4]{0,1:T(4,128)} %param.17) | data formatting | bytes 672 | tf_op args[7]
  3.9 0.1 reshape.53.depart_ref
  4.0 0.1 broadcast_in_dim.11
  4.1 0.1 broadcast_in_dim.13.factor_ref
  4.2 0.0 copy-start
  4.2 1.5 %copy-done = bf16[40,8,1,2688]{3,1,2,0:T(8,128)(2,1)S(1)} copy-done((bf16[40,8,1,2688]{3,1,2,0:T(8,128)(2,1)S(1)}, bf16[40,8,1,2688]{3,1,2,0:T(8,128)(2,1)}, u32[]{:S(2)}) %copy-start) | copy-done | bytes 1720344
  5.7 0.0 copy-start.1
  5.7 0.9 %copy-done.1 = bf16[3,8,1,2688]{3,1,2,0:T(8,128)(2,1)S(1)} copy-done((bf16[3,8,1,2688]{3,1,2,0:T(8,128)(2,1)S(1)}, bf16[3,8,1,2688]{3,1,2,0:T(8,128)(2,1)}, u32[]{:S(2)}) %copy-start.1) | copy-done | bytes 129048
  6.6 0.0 copy-start.2
  6.6 0.0 copy-start.3
  6.6 1.0 %shard_map.121 = (bf16[20,40,8,128]{3,2,1,0:T(8,128)(2,1)S(1)}, bf16[20,3,8,128]{3,2,1,0:T(8,128)(2,1)S(1)}) custom-call(s32[20]{0:T(128)S(1)} %reshape.47.listed_ref, bf16[40,8,2688]{2,1,0:T(8,128)(2,1)S(1)} %bitcast.13, bf16[3,8,2688]{2,1,0:T(8,128)(2,1)S(1)} %bitcast.15), custom_call_target="tpu_custom_call" | custom-call | tf_op jit(solution)/shard_map/pallas_call | solution.py:54
  7.6 0.0 copy-done.4
  7.6 0.0 copy-done.5
  7.6 0.1 copy-done.2
  7.7 0.2 copy-done.3
  8.0 26.7 %shard_map.122 = (bf16[2,8,2688]{2,1,0:T(8,128)(2,1)S(1)}, bf16[20,320,128]{2,1,0:T(8,128)(2,1)S(1)}, bf16[21,512,128]{2,1,0:T(8,128)(2,1)S(1)}) custom-call(bf16[32,80,640]{2,1,0:T(8,128)(2,1)} %bitcast.17, bf16[80,8,640]{2,1,0:T(8,128)(2,1)S(1)} %copy-done.2, bf16[80,8,640]{2,1,0:T(8,128)(2,1)S(1)} %copy-done.3, ...), custom_call_target="tpu_custom_call" | custom-call | flops 4000000000 | bytes 10000000 | tf_op jit(solution)/shard_map/pallas_call | solution.py:449
  34.6 7.0 %shard_map.123 = (bf16[40,8,2688]{2,1,0:T(8,128)(2,1)}, bf16[2,8,2688]{2,1,0:T(8,128)(2,1)}) custom-call(s32[84]{0:T(128)S(1)} %reshape.53.depart_ref, bf16[21,512,128]{2,1,0:T(8,128)(2,1)S(1)} %get-tuple-element.13.stencil_ref, bf16[2,8,2688]{2,1,0:T(8,128)(2,1)S(1)} %get-tuple-element.12.wind_ref, bf16[20,320,128]{2,1,0:T(8,128)(2,1)S(1)} %get-tuple-element.14.pool_ref), custom_call_target="tpu_custom_call" | custom-call | flops 880803840 | bytes 4000000 | tf_op jit(solution)/shard_map/pallas_call | solution.py:89
  41.7 0.6 %copy.25 = bf16[2,8,1,2688]{3,1,2,0:T(8,128)(2,1)} copy(bf16[2,8,1,2688]{3,1,2,0:T(8,128)(2,1)S(1)} %bitcast.14) | data formatting | bytes 172032
  (1 shorter events, 0.0 us)
Async XLA Ops:
  0.6 7.0 %copy-start.4 = (bf16[21,4,4,128]{3,2,1,0:T(4,128)(2,1)S(1)}, bf16[21,4,4,128]{3,2,1,0:T(4,128)(2,1)}, u32[]{:S(2)}) copy-start(bf16[21,4,4,128]{3,2,1,0:T(4,128)(2,1)} %points_ref.1) | copy-start | bytes 258052
  0.6 7.0 %copy-start.5 = (s32[21,4,128]{2,1,0:T(4,128)S(1)}, s32[21,4,128]{2,1,0:T(4,128)}, u32[]{:S(2)}) copy-start(s32[21,4,128]{2,1,0:T(4,128)} %start_ref.1) | copy-start | bytes 129028
  4.2 1.5 %copy-start = (bf16[40,8,1,2688]{3,1,2,0:T(8,128)(2,1)S(1)}, bf16[40,8,1,2688]{3,1,2,0:T(8,128)(2,1)}, u32[]{:S(2)}) copy-start(bf16[40,8,1,2688]{3,1,2,0:T(8,128)(2,1)} %param.14) | copy-start | bytes 5160964
  5.7 0.9 %copy-start.1 = (bf16[3,8,1,2688]{3,1,2,0:T(8,128)(2,1)S(1)}, bf16[3,8,1,2688]{3,1,2,0:T(8,128)(2,1)}, u32[]{:S(2)}) copy-start(bf16[3,8,1,2688]{3,1,2,0:T(8,128)(2,1)} %param.15) | copy-start | bytes 387076
  6.6 1.1 %copy-start.2 = (bf16[80,8,640]{2,1,0:T(8,128)(2,1)S(1)}, bf16[80,8,640]{2,1,0:T(8,128)(2,1)}, u32[]{:S(2)}) copy-start(bf16[80,8,640]{2,1,0:T(8,128)(2,1)} %val_ref.1) | copy-start | bytes 2457604
  6.6 1.4 %copy-start.3 = (bf16[80,8,640]{2,1,0:T(8,128)(2,1)S(1)}, bf16[80,8,640]{2,1,0:T(8,128)(2,1)}, u32[]{:S(2)}) copy-start(bf16[80,8,640]{2,1,0:T(8,128)(2,1)} %slope_ref.1) | copy-start | bytes 2457604

commit v4 on v3

--- a/solution.py
+++ b/solution.py
@@ -38,9 +38,10 @@
 
 def gather_kernel(listed_ref, old_ref, weight_ref, blocks_ref, weights_ref):
     block_count = old_ref.shape[2] // BLK
+    slots = listed_ref.shape[0]
 
     def take(slot, carry):
-        lons = block_of(jnp.clip(listed_ref[slot], 0, block_count - 1))
+        lons = block_of(jnp.clip(listed_ref[slot % slots, slot // slots], 0, block_count - 1))
         blocks_ref[slot] = old_ref[:, :, lons]
         weights_ref[slot] = weight_ref[:, :, lons]
         return carry
@@ -49,7 +50,7 @@
 
 
 def listed_blocks(listed, old, weight):
-    count = listed.shape[0]
+    count = listed.size
     bins, k, _ = old.shape
     return pl.pallas_call(
         gather_kernel,
@@ -69,7 +70,7 @@
     stencil_rows = depth // BLK
 
     def arrive(c, carry):
-        taken = [pool_ref[depart_ref[c * stencil_rows + t]] for t in range(stencil_rows)]
+        taken = [pool_ref[depart_ref[t, c]] for t in range(stencil_rows)]
         new = jnp.dot(
             jnp.concatenate(taken, axis=1), stencil_ref[c], preferred_element_type=jnp.float32
         )
@@ -98,7 +99,7 @@
         cost_estimate=pl.CostEstimate(
             flops=2 * stencil.size * bins * k, bytes_accessed=4_000_000, transcendentals=0
         ),
-    )(depart_slot.reshape(-1), stencil, wind, pool)
+    )(depart_slot.T, stencil, wind, pool)
 
 
 def step_kernel(
@@ -445,7 +446,7 @@
     blocks = pltpu.VMEM((offsets * slots, bins * k, BLK), jnp.bfloat16)
     terms = pltpu.VMEM((bands, rows, lanes), jnp.bfloat16)
     dma = pltpu.SemaphoreType.DMA
-    listed, listed_weight = listed_blocks(send_blocks.reshape(-1), old, weight)
+    listed, listed_weight = listed_blocks(send_blocks[0].T, old, weight)
     wind, pool, stencil = pl.pallas_call(
         functools.partial(step_kernel, (bands, levs, offsets, slots)),
         out_shape=[

time: 42.6 us -> 41.6 us (0.977)
  local copies, waits for them, and re-layouts: 6.05 us -> 4.82 us
    unnamed x15 -> x17, local copies, waits for them, and re-layouts: 4.86 us -> 3.8 us
where the time goes in v4:
time: 41.6 us; the launch traced here: 41.3 us
  Pallas kernels  35 us (84%)
  local copies, waits for them, and re-layouts  4.82 us (12%)
  other arithmetic  0.8 us (2%)
  between operations  0.72 us (2%)
    pallas_call x1, Pallas kernels, shards(): pl.pallas_call(functools.partial(step_kernel, (bands, levs, offsets, slot...  26.7 us
    pallas_call x1, Pallas kernels, arrivals(): pl.pallas_call(arrive_kernel, out_shape=[jax.ShapeDtypeStruct((bins, k, l...  7.07 us
    unnamed x17, local copies, waits for them, and re-layouts  3.8 us
    pallas_call x1, Pallas kernels, listed_blocks(): pl.pallas_call(gather_kernel, out_shape=[jax.ShapeDtypeStruct((count, bin...  1.24 us

profile of v4, /device:TPU:1, one launch (start us, length us, event | category | flops | bytes accessed | tf_op | source)
XLA Modules:
  0.0 41.3 jit_solution(12646052790351990720)
XLA Ops:
  0.6 0.0 copy-start.6
  0.6 0.0 copy-start.7
  0.7 0.8 %convert_multiply_fusion = f32[80]{0:T(128)S(1)} fusion(s32[640]{0:T(1024)} %param.13, s32[]{:T(128)S(6)} %select_n.3), kind=kLoop, calls=%fused_computation | loop fusion | flops 160 | bytes 644 | tf_op jit(solution)/shard_map/div | solution.py:438
  1.5 0.1 broadcast_in_dim.10
  1.5 0.8 %reshape.43 = s32[8,80]{1,0:T(8,128)S(1)} reshape(s32[640]{0:T(1024)} %param.13) | data formatting | bytes 5120 | tf_op jit(solution)/shard_map/reshape | solution.py:441
  2.3 0.1 broadcast_in_dim.11
  2.4 0.1 broadcast_in_dim.13.factor_ref
  2.5 0.0 copy-start
  2.5 1.5 %copy-done = bf16[40,8,1,2688]{3,1,2,0:T(8,128)(2,1)S(1)} copy-done((bf16[40,8,1,2688]{3,1,2,0:T(8,128)(2,1)S(1)}, bf16[40,8,1,2688]{3,1,2,0:T(8,128)(2,1)}, u32[]{:S(2)}) %copy-start) | copy-done | bytes 1720344
  3.9 0.0 copy-start.1
  3.9 0.9 %copy-done.1 = bf16[3,8,1,2688]{3,1,2,0:T(8,128)(2,1)S(1)} copy-done((bf16[3,8,1,2688]{3,1,2,0:T(8,128)(2,1)S(1)}, bf16[3,8,1,2688]{3,1,2,0:T(8,128)(2,1)}, u32[]{:S(2)}) %copy-start.1) | copy-done | bytes 129048
  4.8 0.0 copy-start.2
  4.8 0.7 %copy-done.2 = s32[1,5,4]{1,2,0:T(4,128)S(1)} copy-done((s32[1,5,4]{1,2,0:T(4,128)S(1)}, s32[1,5,4]{1,2,0:T(4,128)}, u32[]{:S(2)}) %copy-start.2) | copy-done | bytes 104
  5.5 0.0 copy-start.4
  5.5 0.0 copy-start.5
  5.5 1.2 %shard_map.121 = (bf16[20,40,8,128]{3,2,1,0:T(8,128)(2,1)S(1)}, bf16[20,3,8,128]{3,2,1,0:T(8,128)(2,1)S(1)}) custom-call(s32[4,5]{1,0:T(4,128)S(1)} %bitcast.21, bf16[40,8,2688]{2,1,0:T(8,128)(2,1)S(1)} %bitcast.17, bf16[3,8,2688]{2,1,0:T(8,128)(2,1)S(1)} %bitcast.19), custom_call_target="tpu_custom_call" | custom-call | tf_op jit(solution)/shard_map/pallas_call | solution.py:55
  6.8 0.0 copy-done.6
  6.8 0.0 copy-done.7
  6.8 0.0 copy-done.4
  6.8 0.1 copy-done.5
  6.9 0.0 copy-start.3
  6.9 26.7 %shard_map.122 = (bf16[2,8,2688]{2,1,0:T(8,128)(2,1)S(1)}, bf16[20,320,128]{2,1,0:T(8,128)(2,1)S(1)}, bf16[21,512,128]{2,1,0:T(8,128)(2,1)S(1)}) custom-call(bf16[32,80,640]{2,1,0:T(8,128)(2,1)} %bitcast.23, bf16[80,8,640]{2,1,0:T(8,128)(2,1)S(1)} %copy-done.4, bf16[80,8,640]{2,1,0:T(8,128)(2,1)S(1)} %copy-done.5, ...), custom_call_target="tpu_custom_call" | custom-call | flops 4000000000 | bytes 10000000 | tf_op jit(solution)/shard_map/pallas_call | solution.py:450
  33.6 0.0 copy-done.3
  33.6 7.1 %shard_map.123 = (bf16[40,8,2688]{2,1,0:T(8,128)(2,1)}, bf16[2,8,2688]{2,1,0:T(8,128)(2,1)}) custom-call(s32[4,21]{1,0:T(4,128)S(1)} %bitcast.22, bf16[21,512,128]{2,1,0:T(8,128)(2,1)S(1)} %get-tuple-element.13.stencil_ref, bf16[2,8,2688]{2,1,0:T(8,128)(2,1)S(1)} %get-tuple-element.12.wind_ref, bf16[20,320,128]{2,1,0:T(8,128)(2,1)S(1)} %get-tuple-element.14.pool_ref), custom_call_target="tpu_custom_call" | custom-call | flops 880803840 | bytes 4000000 | tf_op jit(solution)/shard_map/pallas_call | solution.py:90
  40.7 0.6 %copy.21 = bf16[2,8,1,2688]{3,1,2,0:T(8,128)(2,1)} copy(bf16[2,8,1,2688]{3,1,2,0:T(8,128)(2,1)S(1)} %bitcast.18) | data formatting | bytes 172032
  (1 shorter events, 0.0 us)
Async XLA Ops:
  0.6 6.2 %copy-start.6 = (bf16[21,4,4,128]{3,2,1,0:T(4,128)(2,1)S(1)}, bf16[21,4,4,128]{3,2,1,0:T(4,128)(2,1)}, u32[]{:S(2)}) copy-start(bf16[21,4,4,128]{3,2,1,0:T(4,128)(2,1)} %points_ref.1) | copy-start | bytes 258052
  0.6 6.2 %copy-start.7 = (s32[21,4,128]{2,1,0:T(4,128)S(1)}, s32[21,4,128]{2,1,0:T(4,128)}, u32[]{:S(2)}) copy-start(s32[21,4,128]{2,1,0:T(4,128)} %start_ref.1) | copy-start | bytes 129028
  2.5 1.5 %copy-start = (bf16[40,8,1,2688]{3,1,2,0:T(8,128)(2,1)S(1)}, bf16[40,8,1,2688]{3,1,2,0:T(8,128)(2,1)}, u32[]{:S(2)}) copy-start(bf16[40,8,1,2688]{3,1,2,0:T(8,128)(2,1)} %param.14) | copy-start | bytes 5160964
  3.9 0.9 %copy-start.1 = (bf16[3,8,1,2688]{3,1,2,0:T(8,128)(2,1)S(1)}, bf16[3,8,1,2688]{3,1,2,0:T(8,128)(2,1)}, u32[]{:S(2)}) copy-start(bf16[3,8,1,2688]{3,1,2,0:T(8,128)(2,1)} %param.15) | copy-start | bytes 387076
  4.8 0.7 %copy-start.2 = (s32[1,5,4]{1,2,0:T(4,128)S(1)}, s32[1,5,4]{1,2,0:T(4,128)}, u32[]{:S(2)}) copy-start(s32[1,5,4]{1,2,0:T(4,128)} %param.16) | copy-start | bytes 244
  5.5 1.3 %copy-start.4 = (bf16[80,8,640]{2,1,0:T(8,128)(2,1)S(1)}, bf16[80,8,640]{2,1,0:T(8,128)(2,1)}, u32[]{:S(2)}) copy-start(bf16[80,8,640]{2,1,0:T(8,128)(2,1)} %val_ref.1) | copy-start | bytes 2457604
  5.5 1.4 %copy-start.5 = (bf16[80,8,640]{2,1,0:T(8,128)(2,1)S(1)}, bf16[80,8,640]{2,1,0:T(8,128)(2,1)}, u32[]{:S(2)}) copy-start(bf16[80,8,640]{2,1,0:T(8,128)(2,1)} %slope_ref.1) | copy-start | bytes 2457604
  6.9 26.7 %copy-start.3 = (s32[21,4]{0,1:T(4,128)S(1)}, s32[21,4]{0,1:T(4,128)}, u32[]{:S(2)}) copy-start(s32[21,4]{0,1:T(4,128)} %param.17) | copy-start | bytes 1012
